TPU v7x, 32 devices: a whole 2x2x4 slice. The times are simulated.
32 devices in a mesh: gx: 8 (over z, y), gy: 4 (over x, core).
Axes of the slice: x: 2, y: 2, z: 4, core: 2. Of those that a mesh axis runs over, the one named last changes fastest.
Arguments:
- feats: bfloat16 [8, 4, 16, 512, 128], P('gx', 'gy'), may hold values from -6 to 6
- voxel_mask: int32 [8, 4, 16, 512], P('gx', 'gy'), may hold values 0 or 1
- brick_coord: int32 [8, 4, 16, 3], P('gx', 'gy'), may hold values from 0 to 3, as said below
- brick_count: int32 [8, 4, 2], P('gx', 'gy'), may hold values from 5 to 8, as said below
- route: int32 [8, 4, 16, 2], P('gx', 'gy'), may hold values from 0 to 7, as said below
- conv_weight: bfloat16 [3456, 128], replicated, may hold values from -0.109375 to 0.109375
- down_weight: bfloat16 [1024, 128], replicated, may hold values from -0.1875 to 0.1875
- coarse_grad: bfloat16 [8, 4, 16, 64, 128], P('gx', 'gy'), may hold values from -24 to 24
Outputs:
- coarse: bfloat16 [8, 4, 16, 64, 128], P('gx', 'gy')
- feat_grad: bfloat16 [8, 4, 16, 512, 128], P('gx', 'gy')
- conv_grad: float32 [3456, 128], replicated
- down_grad: float32 [1024, 128], replicated
Inputs may be any that keep to these rules, and one draw needn't show every extreme that they name: `brick_coord`: each slot names a brick position inside its device's tile of 4 x 4 x 4 bricks. The first 8 slots of a device hold distinct positions in the tile's outer brick columns (x or y equal to 0 or 3); the other slots hold distinct positions in the inner columns. `brick_count`: occupied slots come first in each half; some device has all its slots occupied. `route`: all slots of one device have distinct pairs (owner, place), so a device sends at most 2 sub-bricks to one owner; in every gy row one owner receives 2 sub-bricks from every device of the row.
All inputs are finite; a program needn't handle non-finite values. No bound on the sum of `voxel_mask` on one device may be relied on, other than what follows from the above.
Results may differ from a plain program's by a relative error of at most 0.005.
Values may be sent and summed in bfloat16 or wider, within the bound.
A program may use at most 256 MiB of HBM per device.

v0:
```python
import math

import jax
import jax.numpy as jnp
import numpy as np
from jax import lax
from jax.sharding import PartitionSpec as P

CH = 128
EDGE = 8
VOX = 512
TILE = 4
SLOTS = 16
BORDER = 8
CAP = 2


def with_halo(cells, sides, width):
    for axis, dim in sides:
        count = lax.axis_size(axis)
        ends = count - 1
        head = lax.slice_in_dim(cells, 0, width, axis=dim)
        tail = lax.slice_in_dim(cells, cells.shape[dim] - width, cells.shape[dim], axis=dim)
        cells = jnp.concatenate(
            [
                lax.ppermute(tail, axis, [(i, (i + 1) % count) for i in range(ends)]),
                cells,
                lax.ppermute(head, axis, [((i + 1) % count, i) for i in range(ends)]),
            ],
            axis=dim,
        )
    return cells


def tap_offsets():
    return np.array(
        [[a - 1, b - 1, c - 1] for a in range(3) for b in range(3) for c in range(3)],
        dtype=np.int32,
    )


def padded_volume(brick_pool, neighbour_index):
    count = brick_pool.shape[0]
    width = brick_pool.shape[-1]
    voxels = brick_pool.reshape(count, EDGE, EDGE, EDGE, width)
    ranges = [(EDGE - 1, EDGE), (0, EDGE), (0, 1)]
    planes = []
    for a in range(3):
        lines = []
        for b in range(3):
            pieces = []
            for c in range(3):
                sliced = voxels[
                    :,
                    ranges[a][0] : ranges[a][1],
                    ranges[b][0] : ranges[b][1],
                    ranges[c][0] : ranges[c][1],
                ]
                pieces.append(jnp.take(sliced, neighbour_index[:, 9 * a + 3 * b + c], axis=0))
            lines.append(jnp.concatenate(pieces, axis=3))
        planes.append(jnp.concatenate(lines, axis=2))
    return jnp.concatenate(planes, axis=1)


def window_rows(padded, tap):
    a = tap // 9
    b = tap // 3 % 3
    c = tap % 3
    count = padded.shape[0]
    width = padded.shape[-1]
    return padded[:, a : a + EDGE, b : b + EDGE, c : c + EDGE].reshape(count * EDGE**3, width)


def convolve(padded, weight):
    total = None
    for tap in range(27):
        term = jnp.dot(
            window_rows(padded, tap),
            weight[tap * CH : (tap + 1) * CH],
            preferred_element_type=jnp.float32,
        )
        total = term if total is None else total + term
    return total


def pool_pairs(activated):
    count = activated.shape[0]
    half = EDGE // 2
    blocks = activated.reshape(count, half, 2, half, 2, half, 2, CH).transpose(
        0, 1, 3, 5, 2, 4, 6, 7
    )
    return blocks.reshape(count * half**3, 8 * CH)


def unpool_pairs(columns, count):
    half = EDGE // 2
    blocks = columns.reshape(count, half, half, half, 2, 2, 2, CH).transpose(0, 1, 4, 2, 5, 3, 6, 7)
    return blocks.reshape(count, VOX, CH)


def per_device(
    feats, voxel_mask, brick_coord, brick_count, route, conv_weight, down_weight, coarse_grad
):
    tiles_x = lax.axis_size("gx")
    tiles_y = lax.axis_size("gy")
    quarter = VOX // 8
    beside_all = np.array([0, 1, 2, 3, 5, 6, 7, 8], dtype=np.int32)
    slot_ids = jnp.arange(SLOTS, dtype=jnp.int32)
    counts = brick_count[0, 0]
    occupied = jnp.where(slot_ids < BORDER, slot_ids < counts[0], slot_ids - BORDER < counts[1])
    active = voxel_mask[0, 0].astype(jnp.float32) * occupied.astype(jnp.float32)[:, None]
    inputs = feats[0, 0] * active.astype(jnp.bfloat16)[:, :, None]
    coords = brick_coord[0, 0]
    labels = jnp.where(
        occupied, 1 + coords[:, 0] + TILE * coords[:, 1] + TILE * TILE * coords[:, 2], 0
    )[:BORDER]
    outgoing = inputs[:BORDER]
    arrived, arrived_labels = (
        with_halo(outgoing[None, None], (("gx", 0), ("gy", 1)), 1),
        with_halo(labels.astype(jnp.bfloat16)[None, None], (("gx", 0), ("gy", 1)), 1),
    )
    remote = arrived.reshape(9, BORDER, -1, CH)[beside_all].reshape(8 * BORDER, -1, CH)
    remote_labels = arrived_labels.reshape(9, BORDER)[beside_all].astype(jnp.int32)
    packed = remote_labels - 1
    shift_x = jnp.asarray(beside_all // 3 - 1) * TILE
    shift_y = jnp.asarray(beside_all % 3 - 1) * TILE
    far_x = packed % TILE + shift_x[:, None]
    far_y = packed // TILE % TILE + shift_y[:, None]
    far_z = packed // (TILE * TILE)
    cand_x = jnp.concatenate([coords[:, 0], far_x.reshape(-1)])
    cand_y = jnp.concatenate([coords[:, 1], far_y.reshape(-1)])
    cand_z = jnp.concatenate([coords[:, 2], far_z.reshape(-1)])
    cand_live = jnp.concatenate([occupied, (remote_labels > 0).reshape(-1)])
    offsets = jnp.asarray(tap_offsets())
    wanted = coords[:, None, :] + offsets[None]
    matches = (
        (wanted[..., 0:1] == cand_x)
        & (wanted[..., 1:2] == cand_y)
        & (wanted[..., 2:3] == cand_z)
        & cand_live
    )
    cand_total = cand_x.shape[0]
    neighbour_index = jnp.sum(
        jnp.where(matches, jnp.arange(cand_total, dtype=jnp.int32), 0), axis=2
    )
    neighbour_index = neighbour_index + jnp.where(jnp.any(matches, axis=2), 0, cand_total)
    empty_brick = jnp.zeros((1, VOX, CH), jnp.bfloat16)
    brick_pool = jnp.concatenate([inputs, remote, empty_brick], axis=0)
    input_padded = padded_volume(brick_pool, neighbour_index)
    preact = convolve(input_padded, conv_weight).reshape(SLOTS, VOX, CH)
    activated = (jax.nn.silu(preact) * active[..., None]).astype(jnp.bfloat16)
    block_rows = pool_pairs(activated)
    sub_rows = jnp.dot(block_rows, down_weight, preferred_element_type=jnp.float32).astype(
        jnp.bfloat16
    )
    sub_rows = sub_rows.reshape(SLOTS, quarter * CH)
    received_count = CAP * tiles_x
    target = jnp.where(occupied, route[0, 0, :, 0] * CAP + route[0, 0, :, 1], -1)
    placing = (target[None, :] == jnp.arange(received_count, dtype=jnp.int32)[:, None]).astype(
        jnp.bfloat16
    )
    sending = jnp.dot(placing, sub_rows, preferred_element_type=jnp.float32).astype(jnp.bfloat16)
    coarse_block = lax.all_to_all(
        sending.reshape(tiles_x, CAP, quarter * CH), "gx", split_axis=0, concat_axis=0, tiled=True
    ).reshape(received_count, quarter * CH)
    coarse = coarse_block.reshape(1, 1, received_count, quarter, CH)
    returned = lax.all_to_all(
        coarse_grad[0, 0].reshape(tiles_x, CAP, quarter * CH),
        "gx",
        split_axis=0,
        concat_axis=0,
        tiled=True,
    )
    returned = returned.reshape(received_count, quarter * CH)
    grad_rows = lax.dot_general(
        placing, returned, (((0,), (0,)), ((), ())), preferred_element_type=jnp.float32
    ).astype(jnp.bfloat16)
    grad_rows = grad_rows.reshape(SLOTS * quarter, CH)
    down_local = lax.dot_general(
        block_rows, grad_rows, (((0,), (0,)), ((), ())), preferred_element_type=jnp.float32
    )
    back_rows = jnp.dot(grad_rows, down_weight.T, preferred_element_type=jnp.float32)
    grad_act = unpool_pairs(back_rows, SLOTS)
    sigmoid_z = jax.nn.sigmoid(preact)
    grad_pre = (
        grad_act * active[..., None] * sigmoid_z * (1.0 + preact * (1.0 - sigmoid_z))
    ).astype(jnp.bfloat16)
    grad_out = grad_pre[:BORDER]
    grad_arrived = with_halo(grad_out[None, None], (("gx", 0), ("gy", 1)), 1)
    grad_remote = grad_arrived.reshape(9, BORDER, -1, CH)[beside_all].reshape(8 * BORDER, -1, CH)
    grad_pool = jnp.concatenate([grad_pre, grad_remote, empty_brick], axis=0)
    grad_padded = padded_volume(grad_pool, neighbour_index)
    flipped = conv_weight.reshape(27, CH, CH)[::-1].transpose(0, 2, 1).reshape(27 * CH, CH)
    grad_flat = grad_pre.reshape(SLOTS * VOX, CH)
    tap_grads = [
        lax.dot_general(
            window_rows(input_padded, tap),
            grad_flat,
            (((0,), (0,)), ((), ())),
            preferred_element_type=jnp.float32,
        )
        for tap in range(27)
    ]
    conv_local = jnp.concatenate(tap_grads, axis=0)
    back_all = convolve(grad_padded, flipped).reshape(SLOTS, VOX, CH)
    feat_grad = (back_all * active[..., None]).astype(jnp.bfloat16)[None, None]
    conv_sum, down_sum = lax.psum((conv_local, down_local), ("gx", "gy"))
    total_slots = tiles_x * tiles_y * SLOTS
    conv_grad = conv_sum * (1.0 / math.sqrt(total_slots * VOX))
    down_grad = down_sum * (1.0 / math.sqrt(total_slots * VOX // 8))
    return (coarse, feat_grad, conv_grad, down_grad)


def solution(mesh):
    in_specs = (
        P("gx", "gy", None, None, None),
        P("gx", "gy", None, None),
        P("gx", "gy", None, None),
        P("gx", "gy", None),
        P("gx", "gy", None, None),
        P(),
        P(),
        P("gx", "gy", None, None, None),
    )
    out_specs = (P("gx", "gy", None, None, None), P("gx", "gy", None, None, None), P(), P())
    return jax.shard_map(
        per_device, mesh=mesh, in_specs=in_specs, out_specs=out_specs, check_vma=False
    )
```

profile of v0, /device:TPU:0, one launch (start us, length us, event | category | flops | bytes accessed | tf_op | source)
XLA Modules:
  0.0 931.6 jit_solution(10083662530075325596)
XLA Ops:
  31.0 6.9 all-to-all-start.1
  108.4 9.4 %pad_maximum_fusion = bf16[3,3,8,512,128]{4,3,2,1,0:T(8,128)(2,1)} fusion(bf16[3,1,8,512,128]{4,3,2,1,0:T(8,128)(2,1)} %collective-permute-done.3, bf16[1,1,8,512,128]{4,3,2,1,0:T(8,128)(2,1)} %collective-permute-done.1, bf16[1,1,8,512,128]{4,3,2,1,0:T(8,128)(2,1)S(1)} %fusion.5, bf16[1,1,8,512,128]{4,3,2,1,0:T(8,128)(2,1)} %collective-permute-done, ...), kind=kLoop, calls=%fused_computation.111 | loop fusion | flops 18874368 | bytes 18874368 | tf_op jit(solution)/shard_map/concatenate | solution.py:24
  117.8 8.5 gather_fusion
  126.3 16.5 %copy.431 = bf16[64,8,8,8,128]{4,0,3,2,1:T(8,128)(2,1)} copy(bf16[64,8,8,8,128]{4,3,2,1,0:T(8,128)(2,1)} %bitcast.661) | data formatting | bytes 16777216 | tf_op jit(solution)/shard_map/concatenate | solution.py:148
  142.8 7.8 maximum_maximum_fusion
  151.5 7.3 copy.450
  191.8 6.3 gather_fusion.16
  241.9 7.8 maximum_maximum_fusion.7
  249.7 6.2 maximum_maximum_fusion.3
  256.0 18.6 %fusion.47 = (bf16[16,8,8,8,128]{4,3,2,1,0:T(8,128)(2,1)}, bf16[16,8,8,8,128]{4,3,2,1,0:T(8,128)(2,1)}, bf16[16,8,8,8,128]{4,3,2,1,0:T(8,128)(2,1)}, bf16[16,8,8...) fusion(bf16[16,9,10,10,128]{4,3,2,1,0:T(8,128)(2,1)} %maximum_m, ...), kind=kLoop, calls=%fused_computation.507 | loop fusion | bytes 37748736 | tf_op jit(solution)/shard_map/slice | solution.py:71
  274.6 7.8 fusion.52
  321.1 6.4 maximum_maximum_fusion.2
  327.5 18.9 %fusion.48 = (bf16[16,8,8,8,128]{4,3,2,1,0:T(8,128)(2,1)}, bf16[16,8,8,8,128]{4,3,2,1,0:T(8,128)(2,1)}, bf16[16,8,8,8,128]{4,3,2,1,0:T(8,128)(2,1)}, bf16[16,8,8...) fusion(bf16[16,9,10,10,128]{4,3,2,1,0:T(8,128)(2,1)} %maximum_m, ...), kind=kLoop, calls=%fused_computation.508 | loop fusion | bytes 37748736 | tf_op jit(solution)/shard_map/slice | solution.py:71
  348.7 7.9 fusion.51
  401.7 6.3 exponential_add_fusion
  467.3 14.7 %collective-permute-start.10 = (bf16[3,1,8,512,128]{4,2,3,1,0:T(8,128)(2,1)}, bf16[3,1,8,512,128]{4,2,3,1,0:T(8,128)(2,1)}, u32[]{:S(2)}, u32[]{:S(2)}) collective-permute-start(bf16[3,1,8,512,128]{4,2,3,1,0:T(8,128)(2,1)} %pad_maximum_fusion.3), channel_id=1, source_target_pairs={{0,1},{1,2},{2,3},{4,5},{5,6},{6,7},{8,9},{9,10},{10,11},{12,13},{... | collective-permute-start | bytes 9437192 | tf_op jit(solution)/shard_map/ppermute | solution.py:26
  492.3 6.6 all-to-all-start
  498.9 6.1 multiply_convert_fusion.2
  511.6 118.2 %all-reduce.3.cloned.1.call-done = (f32[3456,128]{1,0:T(8,128)}, f32[1024,128]{1,0:T(8,128)}) async-done(((f32[3456,128]{1,0:T(8,128)}, f32[1024,128]{1,0:T(8,128)}), (f32[3456,128]{1,0:T(8,128)}, f32[1024,128]{1,0:T(8,128)})) %all-reduce.3.cloned.1.call-update) | async-done | bytes 2293776 | tf_op jit(solution)/shard_map/psum | solution.py:207
  634.5 8.6 pad_maximum_fusion.1
  643.1 9.9 %copy.486 = bf16[3,3,8,512,128]{4,3,2,1,0:T(8,128)(2,1)} copy(bf16[3,3,8,512,128]{4,2,3,1,0:T(8,128)(2,1)} %pad_maximum_fusion.1) | data formatting | bytes 18874368 | tf_op jit(solution)/shard_map/concatenate | solution.py:24
  653.0 8.8 gather_fusion.2
  661.8 16.5 %copy.487 = bf16[64,8,8,8,128]{4,0,3,2,1:T(8,128)(2,1)} copy(bf16[64,8,8,8,128]{4,3,2,1,0:T(8,128)(2,1)} %bitcast.660) | data formatting | bytes 16777216 | tf_op jit(solution)/shard_map/concatenate | solution.py:191
  678.3 7.6 maximum_maximum_fusion.1
  688.1 7.6 copy.506
  706.9 6.3 gather_fusion.43
  772.2 7.8 maximum_maximum_fusion.9
  780.0 6.2 maximum_maximum_fusion.5
  786.3 18.6 %fusion.45 = (bf16[16,8,8,8,128]{4,3,2,1,0:T(8,128)(2,1)}, bf16[16,8,8,8,128]{4,3,2,1,0:T(8,128)(2,1)}, bf16[16,8,8,8,128]{4,3,2,1,0:T(8,128)(2,1)}, bf16[16,8,8...) fusion(bf16[16,9,10,10,128]{4,3,2,1,0:T(8,128)(2,1)} %maximum_m, ...), kind=kLoop, calls=%fused_computation.505 | loop fusion | bytes 37748736 | tf_op jit(solution)/shard_map/slice | solution.py:71
  804.9 7.8 fusion.50
  852.4 6.2 maximum_maximum_fusion.4
  858.6 18.7 %fusion.46 = (bf16[16,8,8,8,128]{4,3,2,1,0:T(8,128)(2,1)}, bf16[16,8,8,8,128]{4,3,2,1,0:T(8,128)(2,1)}, bf16[16,8,8,8,128]{4,3,2,1,0:T(8,128)(2,1)}, bf16[16,8,8...) fusion(bf16[16,9,10,10,128]{4,3,2,1,0:T(8,128)(2,1)} %maximum_m, ...), kind=kLoop, calls=%fused_computation.506 | loop fusion | bytes 37748736 | tf_op jit(solution)/shard_map/slice | solution.py:71
  (667 shorter events, 496.7 us)
Async XLA Ops:
  7.2 92.8 %copy-start = (bf16[1024,128]{1,0:T(8,128)(2,1)S(1)}, bf16[1024,128]{1,0:T(8,128)(2,1)}, u32[]{:S(2)}) copy-start(bf16[1024,128]{1,0:T(8,128)(2,1)} %param.37) | copy-start | bytes 786436
  7.2 31.4 %copy-start.100 = (s32[1,1,16,512]{3,2,1,0:T(8,128)S(1)}, s32[1,1,16,512]{3,2,1,0:T(8,128)}, u32[]{:S(2)}) copy-start(s32[1,1,16,512]{3,2,1,0:T(8,128)} %param.32) | copy-start | bytes 98308
  7.2 32.0 %copy-start.72 = (bf16[1,1,16,512,128]{4,3,2,1,0:T(8,128)(2,1)S(1)}, bf16[1,1,16,512,128]{4,3,2,1,0:T(8,128)(2,1)}, u32[]{:S(2)}) copy-start(bf16[1,1,16,512,128]{4,3,2,1,0:T(8,128)(2,1)} %param.31) | copy-start | bytes 6291460
  11.9 26.0 %copy-start.145 = (pred[16]{0:T(512)(128)(4,1)}, pred[16]{0:T(512)(128)(4,1)S(1)}, u32[]{:S(2)}) copy-start(pred[16]{0:T(512)(128)(4,1)S(1)} %get-tuple-element.14) | copy-start | bytes 52
  12.5 44.3 %collective-permute-start.4 = (bf16[1,1,8]{2,1,0:T(2,128)(2,1)}, bf16[1,1,8]{2,1,0:T(2,128)(2,1)}, u32[]{:S(2)}, u32[]{:S(2)}) collective-permute-start(bf16[1,1,8]{2,1,0:T(2,128)(2,1)} %slice_bitcast_fusion.136), channel_id=1, source_target_pairs={{0,4},{4,8},{8,12},{12,16},{16,20},{20,24},{24,28},{1,5},{5,9},{9,... | collective-permute-start | bytes 56 | tf_op jit(solution)/shard_map/ppermute | solution.py:26
  17.9 38.8 %collective-permute-start.5 = (bf16[1,1,8]{2,1,0:T(2,128)(2,1)}, bf16[1,1,8]{2,1,0:T(2,128)(2,1)}, u32[]{:S(2)}, u32[]{:S(2)}) collective-permute-start(bf16[1,1,8]{2,1,0:T(2,128)(2,1)} %slice_bitcast_fusion.136), channel_id=1, source_target_pairs={{4,0},{8,4},{12,8},{16,12},{20,16},{24,20},{28,24},{5,1},{9,5},{13... | collective-permute-start | bytes 56 | tf_op jit(solution)/shard_map/ppermute | solution.py:28
  19.2 18.7 %copy-start.139 = (f32[16]{0:T(128)}, f32[16]{0:T(128)S(1)}, u32[]{:S(2)}) copy-start(f32[16]{0:T(128)S(1)} %convert_element_type.87) | copy-start | bytes 196
  22.5 51.3 %collective-permute-start = (bf16[1,1,8,512,128]{4,3,2,1,0:T(8,128)(2,1)S(1)}, bf16[1,1,8,512,128]{4,3,2,1,0:T(8,128)(2,1)}, u32[]{:S(2)}, u32[]{:S(2)}) collective-permute-start(bf16[1,1,8,512,128]{4,3,2,1,0:T(8,128)(2,1)S(1)} %fusion.5), channel_id=1, source_target_pairs={{0,4},{4,8},{8,12},{12,16},{16,20},{20,24},{24,28},{1,5},{5,9},{9,... | collective-permute-start | bytes 3145736 | tf_op jit(solution)/shard_map/ppermute | solution.py:26
  28.0 45.8 %collective-permute-start.1 = (bf16[1,1,8,512,128]{4,3,2,1,0:T(8,128)(2,1)S(1)}, bf16[1,1,8,512,128]{4,3,2,1,0:T(8,128)(2,1)}, u32[]{:S(2)}, u32[]{:S(2)}) collective-permute-start(bf16[1,1,8,512,128]{4,3,2,1,0:T(8,128)(2,1)S(1)} %fusion.5), channel_id=1, source_target_pairs={{4,0},{8,4},{12,8},{16,12},{20,16},{24,20},{28,24},{5,1},{9,5},{13... | collective-permute-start | bytes 3145736 | tf_op jit(solution)/shard_map/ppermute | solution.py:28
  31.0 61.7 %all-to-all-start.1 = ((bf16[8,2,8192]{2,1,0:T(2,128)(2,1)}), bf16[8,2,8192]{2,1,0:T(2,128)(2,1)}, u32[]{:S(2)}, u32[]{:S(2)}) async-start(bf16[8,2,8192]{2,1,0:T(2,128)(2,1)} %reshape_squeeze.3), calls=%async_computation.1 | async-start | bytes 524288 | tf_op jit(solution)/shard_map/all_to_all | solution.py:167
  37.9 591.9 %all-reduce.3.cloned.1.call-start = ((), (), s32[]{:S(2)}) async-start(), calls=%async_computation.2 | async-start | bytes 4587520 | tf_op jit(solution)/shard_map/psum | solution.py:207
  56.1 86.7 %copy-start.142 = (bf16[81]{0:T(256)(128)(2,1)}, bf16[81]{0:T(256)(128)(2,1)S(1)}, u32[]{:S(2)}) copy-start(bf16[81]{0:T(256)(128)(2,1)S(1)} %pad.115.clone) | copy-start | bytes 490
  57.4 2.6 collective-permute-start.6
  58.7 4.8 collective-permute-start.7
  68.6 25.9 %copy-start.135 = (s32[16]{0:T(128)S(1)}, s32[16]{0:T(128)}, u32[]{:S(2)}) copy-start(s32[16]{0:T(128)} %get-tuple-element.12) | copy-start | bytes 196
  77.4 31.0 %collective-permute-start.2 = (bf16[3,1,8,512,128]{4,3,2,1,0:T(8,128)(2,1)}, bf16[3,1,8,512,128]{4,3,2,1,0:T(8,128)(2,1)}, u32[]{:S(2)}, u32[]{:S(2)}) collective-permute-start(bf16[3,1,8,512,128]{4,3,2,1,0:T(8,128)(2,1)} %pad_maximum_fusion.2), channel_id=1, source_target_pairs={{0,1},{1,2},{2,3},{4,5},{5,6},{6,7},{8,9},{9,10},{10,11},{12,13},{... | collective-permute-start | bytes 9437192 | tf_op jit(solution)/shard_map/ppermute | solution.py:26
  80.3 28.1 %collective-permute-start.3 = (bf16[3,1,8,512,128]{4,3,2,1,0:T(8,128)(2,1)}, bf16[3,1,8,512,128]{4,3,2,1,0:T(8,128)(2,1)}, u32[]{:S(2)}, u32[]{:S(2)}) collective-permute-start(bf16[3,1,8,512,128]{4,3,2,1,0:T(8,128)(2,1)} %pad_maximum_fusion.2), channel_id=1, source_target_pairs={{1,0},{2,1},{3,2},{5,4},{6,5},{7,6},{9,8},{10,9},{11,10},{13,12},{... | collective-permute-start | bytes 9437192 | tf_op jit(solution)/shard_map/ppermute | solution.py:28
  200.0 174.9 %copy-start.2 = (bf16[16,8,8,8,128]{4,3,2,1,0:T(8,128)(2,1)}, bf16[16,8,8,8,128]{4,3,2,1,0:T(8,128)(2,1)S(1)}, u32[]{:S(2)}) copy-start(bf16[16,8,8,8,128]{4,3,2,1,0:T(8,128)(2,1)S(1)} %broadcast_select_fusion.1) | copy-start | bytes 6291460
  200.0 21.1 %copy-start.111 = (pred[16]{0:T(512)(128)(4,1)S(1)}, pred[16]{0:T(512)(128)(4,1)}, u32[]{:S(2)}) copy-start(pred[16]{0:T(512)(128)(4,1)} %get-tuple-element.211) | copy-start | bytes 52
  200.0 24.7 %copy-start.95 = (bf16[81,128]{1,0:T(8,128)(2,1)S(1)}, bf16[81,128]{1,0:T(8,128)(2,1)}, u32[]{:S(2)}) copy-start(bf16[81,128]{1,0:T(8,128)(2,1)} %get-tuple-element.104) | copy-start | bytes 62212
  200.0 32.3 %copy-start.110 = (pred[16]{0:T(512)(128)(4,1)S(1)}, pred[16]{0:T(512)(128)(4,1)}, u32[]{:S(2)}) copy-start(pred[16]{0:T(512)(128)(4,1)} %get-tuple-element.209) | copy-start | bytes 52
  284.6 27.2 %copy-start.131 = (pred[16]{0:T(512)(128)(4,1)S(1)}, pred[16]{0:T(512)(128)(4,1)}, u32[]{:S(2)}) copy-start(pred[16]{0:T(512)(128)(4,1)} %get-tuple-element.227) | copy-start | bytes 52
  327.5 18.9 %copy-start.76 = (bf16[3456,128]{1,0:T(8,128)(2,1)S(1)}, bf16[3456,128]{1,0:T(8,128)(2,1)}, u32[]{:S(2)}) copy-start(bf16[3456,128]{1,0:T(8,128)(2,1)} %param.36) | copy-start | bytes 2654212
  401.7 43.2 %copy-start.4 = (f32[8192,128]{1,0:T(8,128)}, f32[8192,128]{1,0:T(8,128)S(1)}, u32[]{:S(2)}) copy-start(f32[8192,128]{1,0:T(8,128)S(1)} %get-tuple-element.251) | copy-start | bytes 12582916
  411.3 52.3 %collective-permute-start.8 = (bf16[1,1,8,512,128]{4,2,3,1,0:T(8,128)(2,1)S(1)}, bf16[1,1,8,512,128]{4,2,3,1,0:T(8,128)(2,1)}, u32[]{:S(2)}, u32[]{:S(2)}) collective-permute-start(bf16[1,1,8,512,128]{4,2,3,1,0:T(8,128)(2,1)S(1)} %fusion.6), channel_id=1, source_target_pairs={{0,4},{4,8},{8,12},{12,16},{16,20},{20,24},{24,28},{1,5},{5,9},{9,... | collective-permute-start | bytes 3145736 | tf_op jit(solution)/shard_map/ppermute | solution.py:26
  416.8 46.8 %collective-permute-start.9 = (bf16[1,1,8,512,128]{4,2,3,1,0:T(8,128)(2,1)S(1)}, bf16[1,1,8,512,128]{4,2,3,1,0:T(8,128)(2,1)}, u32[]{:S(2)}, u32[]{:S(2)}) collective-permute-start(bf16[1,1,8,512,128]{4,2,3,1,0:T(8,128)(2,1)S(1)} %fusion.6), channel_id=1, source_target_pairs={{4,0},{8,4},{12,8},{16,12},{20,16},{24,20},{28,24},{5,1},{9,5},{13... | collective-permute-start | bytes 3145736 | tf_op jit(solution)/shard_map/ppermute | solution.py:28
  463.6 19.9 %copy-start.41 = (bf16[1024,1024]{1,0:T(8,128)(2,1)S(1)}, bf16[1024,1024]{1,0:T(8,128)(2,1)}, u32[]{:S(2)}) copy-start(bf16[1024,1024]{1,0:T(8,128)(2,1)} %reshape.574) | copy-start | bytes 6291460
  467.3 167.1 %collective-permute-start.10 = (bf16[3,1,8,512,128]{4,2,3,1,0:T(8,128)(2,1)}, bf16[3,1,8,512,128]{4,2,3,1,0:T(8,128)(2,1)}, u32[]{:S(2)}, u32[]{:S(2)}) collective-permute-start(bf16[3,1,8,512,128]{4,2,3,1,0:T(8,128)(2,1)} %pad_maximum_fusion.3), channel_id=1, source_target_pairs={{0,1},{1,2},{2,3},{4,5},{5,6},{6,7},{8,9},{9,10},{10,11},{12,13},{... | collective-permute-start | bytes 9437192 | tf_op jit(solution)/shard_map/ppermute | solution.py:26
  482.1 152.4 %collective-permute-start.11 = (bf16[3,1,8,512,128]{4,2,3,1,0:T(8,128)(2,1)}, bf16[3,1,8,512,128]{4,2,3,1,0:T(8,128)(2,1)}, u32[]{:S(2)}, u32[]{:S(2)}) collective-permute-start(bf16[3,1,8,512,128]{4,2,3,1,0:T(8,128)(2,1)} %pad_maximum_fusion.3), channel_id=1, source_target_pairs={{1,0},{2,1},{3,2},{5,4},{6,5},{7,6},{9,8},{10,9},{11,10},{13,12},{... | collective-permute-start | bytes 9437192 | tf_op jit(solution)/shard_map/ppermute | solution.py:28
  492.3 18.4 %all-to-all-start = ((bf16[8,2,8192]{2,1,0:T(2,128)(2,1)}), bf16[8,2,8192]{2,1,0:T(2,128)(2,1)S(1)}, u32[]{:S(2)}, u32[]{:S(2)}) async-start(bf16[8,2,8192]{2,1,0:T(2,128)(2,1)} %reshape.576), calls=%async_computation | async-start | bytes 524288 | tf_op jit(solution)/shard_map/all_to_all | solution.py:163
  727.4 21.0 %copy-start.112 = (pred[16]{0:T(512)(128)(4,1)S(1)}, pred[16]{0:T(512)(128)(4,1)}, u32[]{:S(2)}) copy-start(pred[16]{0:T(512)(128)(4,1)} %get-tuple-element.211) | copy-start | bytes 52
  821.4 21.8 %copy-start.132 = (pred[16]{0:T(512)(128)(4,1)S(1)}, pred[16]{0:T(512)(128)(4,1)}, u32[]{:S(2)}) copy-start(pred[16]{0:T(512)(128)(4,1)} %get-tuple-element.227) | copy-start | bytes 52
  (132 other events, 636.4 us)
Sparse Core Ops, SparseCore 0:
  490.7 139.0 all-reduce.2
where the time goes:
time: 947 us; the launch traced here: 932 us
  local copies, waits for them, and re-layouts  444 us (47%)
  other arithmetic  201 us (21%)
  waiting for transfers between devices  133 us (14%)
  matrix products  80.7 us (9%)
  starting transfers between devices  57.1 us (6%)
  between operations  16.3 us (2%)
    psum x1, waiting for transfers between devices, per_device(): conv_sum, down_sum = lax.psum((conv_local, down_local), ('gx', 'gy'))  118 us
    gather x54, local copies, waits for them, and re-layouts, padded_volume(): jnp.take(sliced, neighbour_index[:, 9 * a + 3 * b + c], axis=0)  105 us
    slice x8, local copies, waits for them, and re-layouts, window_rows(): padded[:, a:a + EDGE, b:b + EDGE, c:c + EDGE]  104 us
    another operation x50, local copies, waits for them, and re-layouts, padded_volume(): jnp.take(sliced, neighbour_index[:, 9 * a + 3 * b + c], axis=0)  64.7 us
    unnamed x303, local copies, waits for them, and re-layouts  57 us
    select_n x54, other arithmetic, padded_volume(): jnp.take(sliced, neighbour_index[:, 9 * a + 3 * b + c], axis=0)  52.1 us
    dot_general x54, matrix products, convolve(): jnp.dot(window_rows(padded, tap), weight[tap * CH:(tap + 1) * CH], prefer...  45.9 us
    ppermute x6, starting transfers between devices, with_halo(): lax.ppermute(tail, axis, [(i, (i + 1) % count) for i in range(ends)])  35.4 us
  transfers between devices with their start and end apart: 15, of which 4 were waited for; matrix products, arithmetic and copies ran while one was open for 12% of the time, Pallas kernels for 0%

commit v1 on v0

v1 whole, which is shorter than its diff:
```python
import math

import jax
import jax.numpy as jnp
import numpy as np
from jax import lax
from jax.experimental import pallas as pl
from jax.experimental.pallas import tpu as pltpu
from jax.sharding import PartitionSpec as P

CH = 128
EDGE = 8
VOX = 512
TILE = 4
SLOTS = 16
BORDER = 8
CAP = 2
SPAN = TILE * EDGE
FACE = SPAN * SPAN
BF = jnp.bfloat16
F32 = jnp.float32
VM = pl.BlockSpec(memory_space=pltpu.VMEM)
SM = pl.BlockSpec(memory_space=pltpu.SMEM)
LIMIT = 60 * 1024 * 1024


def pool_order():
    order = (
        np.arange(VOX).reshape(4, 2, 4, 2, 4, 2).transpose(1, 3, 5, 0, 2, 4).reshape(-1)
    )
    matrix = np.zeros((VOX, VOX), np.float32)
    matrix[np.arange(VOX), order] = 1.0
    return matrix


def put_faces(faces, cube, x, y, z):
    @pl.when(x == 0)
    def _():
        faces[0, pl.ds(y * EDGE, EDGE), z] = cube[0]

    @pl.when(x == TILE - 1)
    def _():
        faces[1, pl.ds(y * EDGE, EDGE), z] = cube[EDGE - 1]

    @pl.when(y == 0)
    def _():
        faces[2, pl.ds(x * EDGE, EDGE), z] = cube[:, 0]

    @pl.when(y == TILE - 1)
    def _():
        faces[3, pl.ds(x * EDGE, EDGE), z] = cube[:, EDGE - 1]


def face_kernel(coord, feats, mask, out, faces):
    faces[...] = jnp.zeros_like(faces)

    def body(s, carry):
        cube = (feats[s].astype(F32) * mask[s].astype(F32)).reshape(EDGE, EDGE, EDGE, CH)
        put_faces(faces, cube, coord[s, 0], coord[s, 1], coord[s, 2])
        return carry

    lax.fori_loop(0, BORDER, body, 0)
    out[...] = faces[...].reshape(4, FACE, CH).astype(BF)


def fill_volume(volume, halo, corners):
    def clear(i, carry):
        volume[i] = jnp.zeros(volume.shape[1:], F32)
        return carry

    lax.fori_loop(0, volume.shape[0], clear, 0)
    inner = slice(1, 1 + SPAN)
    depth = slice(1, 1 + TILE)
    plane = (SPAN, TILE, EDGE, CH)
    volume[0, inner, depth] = halo[0][...].astype(F32).reshape(plane)
    volume[1 + SPAN, inner, depth] = halo[1][...].astype(F32).reshape(plane)
    volume[inner, 0, depth] = halo[2][...].astype(F32).reshape(plane)
    volume[inner, 1 + SPAN, depth] = halo[3][...].astype(F32).reshape(plane)
    for at, (cx, cy) in enumerate(((0, 0), (0, 1), (1, 0), (1, 1))):
        line = corners[at][...].astype(F32).reshape(TILE, EDGE, CH)
        volume[cx * (1 + SPAN), cy * (1 + SPAN), depth] = line


def place_brick(volume, cube, x, y, z):
    volume[pl.ds(1 + x * EDGE, EDGE), pl.ds(1 + y * EDGE, EDGE), 1 + z] = cube


def unfold(volume, shifted, columns, x, y, z):
    ys = pl.ds(y * EDGE, EDGE + 2)
    row = lax.broadcasted_iota(jnp.int32, (EDGE, CH), 0)[None]

    def lines(i, carry):
        at = x * EDGE + i
        mid = volume[at, ys, z + 1]
        low = jnp.where(row == EDGE - 1, volume[at, ys, z], mid)
        high = jnp.where(row == 0, volume[at, ys, z + 2], mid)
        shifted[0, i] = pltpu.roll(low, 1, 1)
        shifted[1, i] = mid
        shifted[2, i] = pltpu.roll(high, EDGE - 1, 1)
        return carry

    lax.fori_loop(0, EDGE + 2, lines, 0, unroll=True)
    for tap in range(27):
        a, b, c = tap // 9, tap // 3 % 3, tap % 3
        piece = shifted[c, a : a + EDGE, b : b + EDGE].reshape(VOX, CH).astype(BF)
        columns[:, tap * CH : (tap + 1) * CH] = piece


def main_kernel(
    coord, target, feats, mask, halo, corners, returned, weight, down, gather, scatter,
    sending, grad_out, face_out, conv_out, down_out,
    volume, shifted, columns, faces, conv_acc, grads, back_rows, blocks,
):
    fill_volume(volume, halo, corners)
    faces[...] = jnp.zeros_like(faces)
    conv_acc[...] = jnp.zeros_like(conv_acc)
    sending[...] = jnp.zeros_like(sending)

    def place(s, carry):
        cube = (feats[s].astype(F32) * mask[s].astype(F32)).reshape(EDGE, EDGE, EDGE, CH)
        place_brick(volume, cube, coord[s, 0], coord[s, 1], coord[s, 2])
        rows = pl.ds(pl.multiple_of(s * 64, 64), 64)
        grads[rows] = returned[target[s]]
        return carry

    lax.fori_loop(0, SLOTS, place, 0)

    def spread(i, carry):
        rows = pl.ds(pl.multiple_of(i * 256, 256), 256)
        back_rows[rows] = lax.dot_general(
            grads[rows], down[...], (((1,), (1,)), ((), ())), preferred_element_type=F32
        )
        return carry

    lax.fori_loop(0, SLOTS // 4, spread, 0)

    def body(s, carry):
        x, y, z = coord[s, 0], coord[s, 1], coord[s, 2]
        rows = pl.ds(pl.multiple_of(s * 64, 64), 64)
        unfold(volume, shifted, columns, x, y, z)
        preact = jnp.dot(columns[...], weight[...], preferred_element_type=F32)
        active = mask[s].astype(F32)
        sig = jax.nn.sigmoid(preact)
        activated = (preact * sig * active).astype(BF)
        ordered = jnp.dot(gather[...], activated, preferred_element_type=F32).astype(BF)
        blocks[rows] = jnp.concatenate([ordered[64 * q : 64 * q + 64] for q in range(8)], axis=1)
        wide = back_rows[rows]
        tall = jnp.concatenate([wide[:, CH * q : CH * q + CH] for q in range(8)], axis=0)
        head = tall.astype(BF)
        rest = (tall - head.astype(F32)).astype(BF)
        both = jnp.dot(
            scatter[...], jnp.concatenate([head, rest], axis=1), preferred_element_type=F32
        )
        grad_act = both[:, :CH] + both[:, CH:]
        grad_f32 = grad_act * active * sig * (1.0 + preact * (1.0 - sig))
        grad = grad_f32.astype(BF)
        grad_out[s] = grad
        rounded = grad.astype(F32)

        @pl.when(s < BORDER)
        def _():
            put_faces(faces, rounded.reshape(EDGE, EDGE, EDGE, CH), x, y, z)

        turned = rounded.T.astype(BF)
        conv_acc[...] += jnp.dot(turned, columns[...], preferred_element_type=F32)
        return carry

    lax.fori_loop(0, SLOTS, body, 0)
    face_out[...] = faces[...].reshape(4, FACE, CH).astype(BF)
    for tap in range(27):
        conv_out[tap * CH : (tap + 1) * CH] = conv_acc[:, tap * CH : (tap + 1) * CH].T
    turned = grads[...].astype(F32).T.astype(BF)
    down_acc = jnp.dot(turned, blocks[...], preferred_element_type=F32)
    for q in range(8):
        down_out[q * CH : (q + 1) * CH] = down_acc[:, q * CH : (q + 1) * CH].T

    def send(s, carry):
        rows = pl.ds(pl.multiple_of(s * 64, 64), 64)
        sub = jnp.dot(blocks[rows], down[...], preferred_element_type=F32)
        sending[target[s]] = sub.astype(BF)
        return carry

    lax.fori_loop(0, SLOTS, send, 0)


def back_kernel(coord, grad, mask, halo, corners, weight, out, volume, shifted, columns):
    fill_volume(volume, halo, corners)

    def place(s, carry):
        cube = grad[s].astype(F32).reshape(EDGE, EDGE, EDGE, CH)
        place_brick(volume, cube, coord[s, 0], coord[s, 1], coord[s, 2])
        return carry

    lax.fori_loop(0, SLOTS, place, 0)

    def body(s, carry):
        unfold(volume, shifted, columns, coord[s, 0], coord[s, 1], coord[s, 2])
        back = jnp.dot(columns[...], weight[...], preferred_element_type=F32)
        out[s] = (back * mask[s].astype(F32)).astype(BF)
        return carry

    lax.fori_loop(0, SLOTS, body, 0)


VOLUME = pltpu.VMEM((SPAN + 2, SPAN + 2, TILE + 2, EDGE, CH), F32)
SHIFTED = pltpu.VMEM((3, EDGE + 2, EDGE + 2, EDGE, CH), F32)
COLUMNS = pltpu.VMEM((VOX, 27 * CH), BF)
FACES = pltpu.VMEM((4, SPAN, TILE, EDGE, CH), F32)


def swap_faces(faces):
    nx, ny = lax.axis_size("gx"), lax.axis_size("gy")
    up_x = [(i, i + 1) for i in range(nx - 1)]
    down_x = [(i + 1, i) for i in range(nx - 1)]
    up_y = [(j, j + 1) for j in range(ny - 1)]
    down_y = [(j + 1, j) for j in range(ny - 1)]
    halo = (
        lax.ppermute(faces[1], "gx", up_x),
        lax.ppermute(faces[0], "gx", down_x),
        lax.ppermute(faces[3], "gy", up_y),
        lax.ppermute(faces[2], "gy", down_y),
    )
    corners = []
    for cx in (0, 1):
        for cy in (0, 1):
            line = faces[1 - cx, FACE - SPAN :] if cy == 0 else faces[1 - cx, :SPAN]
            pairs = [
                (i * ny + j, (i + 1 - 2 * cx) * ny + j + 1 - 2 * cy)
                for i in range(nx)
                for j in range(ny)
                if 0 <= i + 1 - 2 * cx < nx and 0 <= j + 1 - 2 * cy < ny
            ]
            corners.append(lax.ppermute(line, ("gx", "gy"), pairs))
    return halo, corners


def unpack(kernel, at):
    def wrapped(*refs):
        kernel(*refs[:at], refs[at : at + 4], refs[at + 4 : at + 8], *refs[at + 8 :])

    return wrapped


def per_device(
    feats, voxel_mask, brick_coord, brick_count, route, conv_weight, down_weight, coarse_grad
):
    tiles_x = lax.axis_size("gx")
    tiles_y = lax.axis_size("gy")
    quarter = VOX // 8
    received = CAP * tiles_x
    params = pltpu.CompilerParams(vmem_limit_bytes=LIMIT)
    slot_ids = jnp.arange(SLOTS, dtype=jnp.int32)
    counts = brick_count[0, 0]
    occupied = jnp.where(slot_ids < BORDER, slot_ids < counts[0], slot_ids - BORDER < counts[1])
    mask = jnp.broadcast_to(
        jnp.where(occupied[:, None], voxel_mask[0, 0], 0).astype(BF)[:, :, None], (SLOTS, VOX, CH)
    )
    coord = brick_coord[0, 0]
    target = route[0, 0, :, 0] * CAP + route[0, 0, :, 1]
    feats = feats[0, 0]

    faces = pl.pallas_call(
        face_kernel,
        out_shape=jax.ShapeDtypeStruct((4, FACE, CH), BF),
        in_specs=[SM, VM, VM],
        out_specs=VM,
        scratch_shapes=[FACES],
        compiler_params=params,
    )(coord, feats, mask)
    returned = lax.all_to_all(
        coarse_grad[0, 0].reshape(tiles_x, CAP * quarter, CH),
        "gx", split_axis=0, concat_axis=0, tiled=True,
    ).reshape(received, quarter, CH)
    halo, corners = swap_faces(faces)
    order = pool_order()
    sending, grad_pre, grad_faces, conv_local, down_local = pl.pallas_call(
        unpack(main_kernel, 4),
        out_shape=(
            jax.ShapeDtypeStruct((received, quarter, CH), BF),
            jax.ShapeDtypeStruct((SLOTS, VOX, CH), BF),
            jax.ShapeDtypeStruct((4, FACE, CH), BF),
            jax.ShapeDtypeStruct((27 * CH, CH), F32),
            jax.ShapeDtypeStruct((8 * CH, CH), F32),
        ),
        in_specs=[SM, SM] + [VM] * 15,
        out_specs=(VM,) * 5,
        scratch_shapes=[
            VOLUME, SHIFTED, COLUMNS, FACES,
            pltpu.VMEM((CH, 27 * CH), F32),
            pltpu.VMEM((SLOTS * quarter, CH), BF),
            pltpu.VMEM((SLOTS * quarter, 8 * CH), F32),
            pltpu.VMEM((SLOTS * quarter, 8 * CH), BF),
        ],
        compiler_params=params,
        cost_estimate=pl.CostEstimate(
            flops=4 * SLOTS * VOX * 27 * CH * CH, bytes_accessed=16 << 20, transcendentals=0
        ),
    )(
        coord, target, feats, mask, *halo, *corners, returned, conv_weight, down_weight,
        jnp.asarray(order, BF), jnp.asarray(order.T, BF),
    )
    conv_sum, down_sum = lax.psum((conv_local, down_local), ("gx", "gy"))
    grad_halo, grad_corners = swap_faces(grad_faces)
    coarse = lax.all_to_all(
        sending.reshape(tiles_x, CAP * quarter, CH), "gx", split_axis=0, concat_axis=0, tiled=True
    ).reshape(1, 1, received, quarter, CH)
    flipped = conv_weight.reshape(27, CH, CH)[::-1].transpose(0, 2, 1).reshape(27 * CH, CH)
    feat_grad = pl.pallas_call(
        unpack(back_kernel, 3),
        out_shape=jax.ShapeDtypeStruct((SLOTS, VOX, CH), BF),
        in_specs=[SM] + [VM] * 11,
        out_specs=VM,
        scratch_shapes=[VOLUME, SHIFTED, COLUMNS],
        compiler_params=params,
        cost_estimate=pl.CostEstimate(
            flops=2 * SLOTS * VOX * 27 * CH * CH, bytes_accessed=8 << 20, transcendentals=0
        ),
    )(coord, grad_pre, mask, *grad_halo, *grad_corners, flipped)
    total_slots = tiles_x * tiles_y * SLOTS
    conv_grad = conv_sum * (1.0 / math.sqrt(total_slots * VOX))
    down_grad = down_sum * (1.0 / math.sqrt(total_slots * VOX // 8))
    return (coarse, feat_grad[None, None], conv_grad, down_grad)


def solution(mesh):
    in_specs = (
        P("gx", "gy", None, None, None),
        P("gx", "gy", None, None),
        P("gx", "gy", None, None),
        P("gx", "gy", None),
        P("gx", "gy", None, None),
        P(),
        P(),
        P("gx", "gy", None, None, None),
    )
    out_specs = (P("gx", "gy", None, None, None), P("gx", "gy", None, None, None), P(), P())
    return jax.shard_map(
        per_device, mesh=mesh, in_specs=in_specs, out_specs=out_specs, check_vma=False
    )
```

time: 947 us -> 286 us (0.30); the launches traced: 932 us -> 285 us
  local copies, waits for them, and re-layouts: 444 us -> 12.9 us
  other arithmetic: 201 us -> 6.4 us
  Pallas kernels: 0 us -> 105 us
  matrix products: 80.7 us -> 0 us
  waiting for transfers between devices: 133 us -> 87.7 us
    gather x57 -> x0, local copies, waits for them, and re-layouts: 123 us -> none  [the longest x54 105 us: padded_volume(): jnp.take(sliced, neighbour_index[:, 9 * a + 3 * b + c], axis=0)]
    slice x10 -> x0, local copies, waits for them, and re-layouts: 105 us -> none  [the longest x8 104 us: window_rows(): padded[:, a:a + EDGE, b:b + EDGE, c:c + EDGE]]
    pallas_call x0 -> x3, Pallas kernels: none -> 105 us  [the longest x1 72.7 us: per_device(): pl.pallas_call(unpack(main_kernel, 4), out_shape=(jax.ShapeDtypeStruct((r...]
    concatenate x26 -> x0, other arithmetic: 99.3 us -> none  [the longest x6 26.7 us: with_halo(): jnp.concatenate([lax.ppermute(tail, axis, [(i, (i + 1) % count) for i in...]
    dot_general x86 -> x0, matrix products: 80.7 us -> none  [the longest x54 45.9 us: convolve(): jnp.dot(window_rows(padded, tap), weight[tap * CH:(tap + 1) * CH], prefer...]
    another operation x52 -> x0, local copies, waits for them, and re-layouts: 67.3 us -> none  [the longest x50 64.7 us: padded_volume(): jnp.take(sliced, neighbour_index[:, 9 * a + 3 * b + c], axis=0)]
    concatenate x6 -> x0, local copies, waits for them, and re-layouts: 57.8 us -> none  [the longest x2 24 us: per_device(): grad_pool = jnp.concatenate([grad_pre, grad_remote, empty_brick], axis=0)]
    psum x1, waiting for transfers between devices: 118 us -> 64.7 us  [per_device(): conv_sum, down_sum = lax.psum((conv_local, down_local), ('gx', 'gy'))]
  transfers between devices with their start and end apart: 15 -> 19, of which waited for: 4 -> 4; matrix products, arithmetic and copies ran while one was open for 12% -> 1% of each run, Pallas kernels for 0% -> 10%
where the time goes in v1:
time: 286 us; the launch traced here: 285 us
  Pallas kernels  105 us (37%)
  waiting for transfers between devices  87.7 us (31%)
  starting transfers between devices  58.8 us (21%)
  between operations  14.4 us (5%)
  local copies, waits for them, and re-layouts  12.9 us (5%)
  other arithmetic  6.4 us (2%)
    pallas_call x1, Pallas kernels, per_device(): pl.pallas_call(unpack(main_kernel, 4), out_shape=(jax.ShapeDtypeStruct((r...  72.7 us
    psum x1, waiting for transfers between devices, per_device(): conv_sum, down_sum = lax.psum((conv_local, down_local), ('gx', 'gy'))  64.7 us
    pallas_call x1, Pallas kernels, per_device(): pl.pallas_call(unpack(back_kernel, 3), out_shape=jax.ShapeDtypeStruct((SL...  28.1 us
    ppermute x8, waiting for transfers between devices, swap_faces(): corners.append(lax.ppermute(line, ('gx', 'gy'), pairs))  22.9 us
    ppermute x8, starting transfers between devices, swap_faces(): corners.append(lax.ppermute(line, ('gx', 'gy'), pairs))  16.1 us
    all_to_all x1, starting transfers between devices, per_device(): lax.all_to_all(sending.reshape(tiles_x, CAP * quarter, CH), 'gx', split_a...  15.3 us
    ppermute x2, starting transfers between devices, swap_faces(): lax.ppermute(faces[1], 'gx', up_x)  9.88 us
    all_to_all x1, starting transfers between devices, per_device(): lax.all_to_all(coarse_grad[0, 0].reshape(tiles_x, CAP * quarter, CH), 'gx...  6.8 us
  transfers between devices with their start and end apart: 19, of which 4 were waited for; matrix products, arithmetic and copies ran while one was open for 1% of the time, Pallas kernels for 10%

profile of v1, /device:TPU:0, one launch (start us, length us, event | category | flops | bytes accessed | tf_op | source)
XLA Modules:
  0.0 284.8 jit_solution(10854189896021569165)
XLA Ops:
  7.2 1.3 fusion.1
  8.5 1.4 copy.18
  9.8 1.3 compare_select_fusion
  11.1 0.8 fusion
  12.0 2.2 broadcast_in_dim.24.mask.refs_3_.refs_2_
  14.2 3.7 %shard_map.129 = bf16[4,1024,128]{2,1,0:T(8,128)(2,1)} custom-call(s32[16,3]{1,0:T(8,128)} %bitcast.57, bf16[16,512,128]{2,1,0:T(8,128)(2,1)} %bitcast.51, bf16[16,512,128]{2,1,0:T(8,128)(2,1)} %broadcast_in_dim.24.mask.refs_3_.refs_2_), custom_call_target="tpu_custom_call" | custom-call | tf_op jit(solution)/shard_map/pallas_call | solution.py:262
  17.9 1.3 slice_bitcast_fusion
  19.2 4.9 %collective-permute-start = (bf16[1024,128]{1,0:T(8,128)(2,1)S(1)}, bf16[1024,128]{1,0:T(8,128)(2,1)S(1)}, u32[]{:S(2)}, u32[]{:S(2)}) collective-permute-start(bf16[1024,128]{1,0:T(8,128)(2,1)S(1)} %get-tuple-element.31), channel_id=1, source_target_pairs={{0,4},{4,8},{8,12},{12,16},{16,20},{20,24},{24,28},{1,5},{5,9},{9,... | collective-permute-start | bytes 786440 | tf_op jit(solution)/shard_map/ppermute | solution.py:218
  24.1 1.3 collective-permute-start.1
  25.4 1.5 collective-permute-start.2
  26.9 1.3 collective-permute-start.3
  28.2 6.8 %all-to-all-start = ((bf16[8,128,128]{2,1,0:T(8,128)(2,1)}), bf16[8,128,128]{2,1,0:T(8,128)(2,1)S(1)}, u32[]{:S(2)}, u32[]{:S(2)}) async-start(bf16[8,128,128]{2,1,0:T(8,128)(2,1)} %bitcast.14), calls=%async_computation | async-start | bytes 524288 | tf_op jit(solution)/shard_map/all_to_all | solution.py:270
  35.8 5.7 %collective-permute-start.4 = (bf16[32,128]{1,0:T(8,128)(2,1)S(1)}, bf16[32,128]{1,0:T(8,128)(2,1)S(1)}, u32[]{:S(2)}, u32[]{:S(2)}) collective-permute-start(bf16[32,128]{1,0:T(8,128)(2,1)S(1)} %get-tuple-element.27), channel_id=1, source_target_pairs={{0,5},{1,6},{2,7},{4,9},{5,10},{6,11},{8,13},{9,14},{10,15},{12,17... | collective-permute-start | bytes 24584 | tf_op jit(solution)/shard_map/ppermute | solution.py:233
  41.5 1.3 collective-permute-done.4.refs_8_
  44.2 1.3 collective-permute-start.7
  46.1 14.3 %collective-permute-done.7.refs_11_ = bf16[32,128]{1,0:T(8,128)(2,1)S(1)} collective-permute-done((bf16[32,128]{1,0:T(8,128)(2,1)S(1)}, bf16[32,128]{1,0:T(8,128)(2,1)S(1)}, u32[]{:S(2)}, u32[]{:S(2)}) %collective-permute-start.7) | collective-permute-done | bytes 8224 | tf_op jit(solution)/shard_map/ppermute | solution.py:233
  61.5 72.7 %shard_map.130 = (bf16[16,64,128]{2,1,0:T(8,128)(2,1)}, bf16[16,512,128]{2,1,0:T(8,128)(2,1)}, bf16[4,1024,128]{2,1,0:T(8,128)(2,1)}, f32[3456,128]{1,0:T(8,128)}, f32[1024,128]{1,0:T(8,128)}) custom-call(s32[16,3]{1,0:T(8,128)} %bitcast.58, s32[16]{0:T(128)} %add_bitcast_fusion.refs_1_, bf16[16,512,128]{2,1,0:T(8,128)(2,1)} %bitcast.52, ...), custom_call_target="tpu_custom_call" | custom-call | flops 14495514624 | bytes 16777216 | tf_op jit(solution)/shard_map/pallas_call | solution.py:276
  134.2 1.2 copy-done
  135.4 4.1 %collective-permute-start.10 = (bf16[1024,128]{1,0:T(8,128)(2,1)S(1)}, bf16[1024,128]{1,0:T(8,128)(2,1)S(1)}, u32[]{:S(2)}, u32[]{:S(2)}) collective-permute-start(bf16[1024,128]{1,0:T(8,128)(2,1)S(1)} %get-tuple-element.21), channel_id=1, source_target_pairs={{0,1},{1,2},{2,3},{4,5},{5,6},{6,7},{8,9},{9,10},{10,11},{12,13},{... | collective-permute-start | bytes 786440 | tf_op jit(solution)/shard_map/ppermute | solution.py:220
  139.5 1.3 collective-permute-start.11
  140.8 5.0 %collective-permute-start.8 = (bf16[1024,128]{1,0:T(8,128)(2,1)S(1)}, bf16[1024,128]{1,0:T(8,128)(2,1)}, u32[]{:S(2)}, u32[]{:S(2)}) collective-permute-start(bf16[1024,128]{1,0:T(8,128)(2,1)S(1)} %get-tuple-element.23), channel_id=1, source_target_pairs={{0,4},{4,8},{8,12},{12,16},{16,20},{20,24},{24,28},{1,5},{5,9},{9,... | collective-permute-start | bytes 786440 | tf_op jit(solution)/shard_map/ppermute | solution.py:218
  145.8 1.3 collective-permute-start.9
  147.1 5.1 %collective-permute-start.12 = (bf16[32,128]{1,0:T(8,128)(2,1)S(1)}, bf16[32,128]{1,0:T(8,128)(2,1)S(1)}, u32[]{:S(2)}, u32[]{:S(2)}) collective-permute-start(bf16[32,128]{1,0:T(8,128)(2,1)S(1)} %get-tuple-element.19), channel_id=1, source_target_pairs={{0,5},{1,6},{2,7},{4,9},{5,10},{6,11},{8,13},{9,14},{10,15},{12,17... | collective-permute-start | bytes 24584 | tf_op jit(solution)/shard_map/ppermute | solution.py:233
  152.3 7.2 %collective-permute-done.12.refs_7_ = bf16[32,128]{1,0:T(8,128)(2,1)S(1)} collective-permute-done((bf16[32,128]{1,0:T(8,128)(2,1)S(1)}, bf16[32,128]{1,0:T(8,128)(2,1)S(1)}, u32[]{:S(2)}, u32[]{:S(2)}) %collective-permute-start.12) | collective-permute-done | bytes 8224 | tf_op jit(solution)/shard_map/ppermute | solution.py:233
  160.9 1.3 collective-permute-start.15
  162.2 1.3 copy.16
  163.5 1.0 rev.3
  164.5 15.3 %all-to-all-start.1 = ((bf16[8,128,128]{2,1,0:T(8,128)(2,1)}), bf16[8,128,128]{2,1,0:T(8,128)(2,1)S(1)}, u32[]{:S(2)}, u32[]{:S(2)}) async-start(bf16[8,128,128]{2,1,0:T(8,128)(2,1)} %bitcast.16), calls=%async_computation.1 | async-start | bytes 524288 | tf_op jit(solution)/shard_map/all_to_all | solution.py:304
  180.7 28.1 %shard_map.131 = bf16[16,512,128]{2,1,0:T(8,128)(2,1)} custom-call(s32[16,3]{1,0:T(8,128)} %bitcast.59, bf16[16,512,128]{2,1,0:T(8,128)(2,1)} %get-tuple-element.10.refs_1_, bf16[16,512,128]{2,1,0:T(8,128)(2,1)} %broadcast_in_dim.24.mask.refs_3_.refs_2_, bf16[1024,128]{1,0:T(8,128)(2,1)} %collective-permute-done.8.refs_3_, ...), custom_call_target="tpu_custom_call" | custom-call | flops 7247757312 | bytes 8388608 | tf_op jit(solution)/shard_map/pallas_call | solution.py:308
  208.8 64.7 %all-reduce.3.cloned.1.call-done = (f32[3456,128]{1,0:T(8,128)}, f32[1024,128]{1,0:T(8,128)}) async-done(((f32[3456,128]{1,0:T(8,128)}, f32[1024,128]{1,0:T(8,128)}), (f32[3456,128]{1,0:T(8,128)}, f32[1024,128]{1,0:T(8,128)})) %all-reduce.3.cloned.1.call-update) | async-done | bytes 2293776 | tf_op jit(solution)/shard_map/psum | solution.py:302
  273.5 2.9 %broadcast_multiply_fusion = f32[3456,128]{1,0:T(8,128)} fusion(f32[3456,128]{1,0:T(8,128)} %get-tuple-element.14), kind=kLoop, calls=%fused_computation | loop fusion | flops 442368 | bytes 3538944 | tf_op jit(solution)/shard_map/mul | solution.py:320
  276.4 0.8 broadcast_multiply_fusion.1
  (63 shorter events, 6.6 us)
Async XLA Ops:
  17.9 27.6 %copy-start.18 = (s32[1,1,16,2]{2,3,1,0:T(2,128)S(1)}, s32[1,1,16,2]{2,3,1,0:T(2,128)}, u32[]{:S(2)}) copy-start(s32[1,1,16,2]{2,3,1,0:T(2,128)} %param.14) | copy-start | bytes 388
  19.2 41.3 %collective-permute-start = (bf16[1024,128]{1,0:T(8,128)(2,1)S(1)}, bf16[1024,128]{1,0:T(8,128)(2,1)S(1)}, u32[]{:S(2)}, u32[]{:S(2)}) collective-permute-start(bf16[1024,128]{1,0:T(8,128)(2,1)S(1)} %get-tuple-element.31), channel_id=1, source_target_pairs={{0,4},{4,8},{8,12},{12,16},{16,20},{20,24},{24,28},{1,5},{5,9},{9,... | collective-permute-start | bytes 786440 | tf_op jit(solution)/shard_map/ppermute | solution.py:218
  24.1 36.4 %collective-permute-start.1 = (bf16[1024,128]{1,0:T(8,128)(2,1)S(1)}, bf16[1024,128]{1,0:T(8,128)(2,1)S(1)}, u32[]{:S(2)}, u32[]{:S(2)}) collective-permute-start(bf16[1024,128]{1,0:T(8,128)(2,1)S(1)} %get-tuple-element.30), channel_id=1, source_target_pairs={{4,0},{8,4},{12,8},{16,12},{20,16},{24,20},{28,24},{5,1},{9,5},{13... | collective-permute-start | bytes 786440 | tf_op jit(solution)/shard_map/ppermute | solution.py:219
  25.4 35.1 %collective-permute-start.2 = (bf16[1024,128]{1,0:T(8,128)(2,1)S(1)}, bf16[1024,128]{1,0:T(8,128)(2,1)S(1)}, u32[]{:S(2)}, u32[]{:S(2)}) collective-permute-start(bf16[1024,128]{1,0:T(8,128)(2,1)S(1)} %get-tuple-element.29), channel_id=1, source_target_pairs={{0,1},{1,2},{2,3},{4,5},{5,6},{6,7},{8,9},{9,10},{10,11},{12,13},{... | collective-permute-start | bytes 786440 | tf_op jit(solution)/shard_map/ppermute | solution.py:220
  26.9 33.6 %collective-permute-start.3 = (bf16[1024,128]{1,0:T(8,128)(2,1)S(1)}, bf16[1024,128]{1,0:T(8,128)(2,1)S(1)}, u32[]{:S(2)}, u32[]{:S(2)}) collective-permute-start(bf16[1024,128]{1,0:T(8,128)(2,1)S(1)} %get-tuple-element.28), channel_id=1, source_target_pairs={{1,0},{2,1},{3,2},{5,4},{6,5},{7,6},{9,8},{10,9},{11,10},{13,12},{... | collective-permute-start | bytes 786440 | tf_op jit(solution)/shard_map/ppermute | solution.py:221
  28.2 32.3 %all-to-all-start = ((bf16[8,128,128]{2,1,0:T(8,128)(2,1)}), bf16[8,128,128]{2,1,0:T(8,128)(2,1)S(1)}, u32[]{:S(2)}, u32[]{:S(2)}) async-start(bf16[8,128,128]{2,1,0:T(8,128)(2,1)} %bitcast.14), calls=%async_computation | async-start | bytes 524288 | tf_op jit(solution)/shard_map/all_to_all | solution.py:270
  35.0 238.6 %all-reduce.3.cloned.1.call-start = ((), (), s32[]{:S(2)}) async-start(), calls=%async_computation.2 | async-start | bytes 4587520 | tf_op jit(solution)/shard_map/psum | solution.py:302
  35.8 7.1 %collective-permute-start.4 = (bf16[32,128]{1,0:T(8,128)(2,1)S(1)}, bf16[32,128]{1,0:T(8,128)(2,1)S(1)}, u32[]{:S(2)}, u32[]{:S(2)}) collective-permute-start(bf16[32,128]{1,0:T(8,128)(2,1)S(1)} %get-tuple-element.27), channel_id=1, source_target_pairs={{0,5},{1,6},{2,7},{4,9},{5,10},{6,11},{8,13},{9,14},{10,15},{12,17... | collective-permute-start | bytes 24584 | tf_op jit(solution)/shard_map/ppermute | solution.py:233
  42.9 17.7 %copy-start.10 = (bf16[32,128]{1,0:T(8,128)(2,1)}, bf16[32,128]{1,0:T(8,128)(2,1)S(1)}, u32[]{:S(2)}) copy-start(bf16[32,128]{1,0:T(8,128)(2,1)S(1)} %collective-permute-done.4.refs_8_) | copy-start | bytes 24580
  42.9 0.7 collective-permute-start.5
  43.5 17.0 %copy-start.12 = (bf16[32,128]{1,0:T(8,128)(2,1)}, bf16[32,128]{1,0:T(8,128)(2,1)S(1)}, u32[]{:S(2)}) copy-start(bf16[32,128]{1,0:T(8,128)(2,1)S(1)} %collective-permute-done.5.refs_9_) | copy-start | bytes 24580
  43.5 0.7 collective-permute-start.6
  44.2 16.3 %copy-start.14 = (bf16[32,128]{1,0:T(8,128)(2,1)}, bf16[32,128]{1,0:T(8,128)(2,1)S(1)}, u32[]{:S(2)}) copy-start(bf16[32,128]{1,0:T(8,128)(2,1)S(1)} %collective-permute-done.6.refs_10_) | copy-start | bytes 24580
  44.2 16.2 %collective-permute-start.7 = (bf16[32,128]{1,0:T(8,128)(2,1)S(1)}, bf16[32,128]{1,0:T(8,128)(2,1)S(1)}, u32[]{:S(2)}, u32[]{:S(2)}) collective-permute-start(bf16[32,128]{1,0:T(8,128)(2,1)S(1)} %get-tuple-element.24), channel_id=1, source_target_pairs={{5,0},{6,1},{7,2},{9,4},{10,5},{11,6},{13,8},{14,9},{15,10},{17,12... | collective-permute-start | bytes 24584 | tf_op jit(solution)/shard_map/ppermute | solution.py:233
  60.5 0.9 copy-start.6
  60.5 0.9 copy-start.8
  60.5 1.0 copy-start.3
  134.1 1.2 copy-start
  134.2 28.0 %copy-start.1 = (bf16[3456,128]{1,0:T(8,128)(2,1)S(1)}, bf16[3456,128]{1,0:T(8,128)(2,1)}, u32[]{:S(2)}) copy-start(bf16[3456,128]{1,0:T(8,128)(2,1)} %refs_13_.1) | copy-start | bytes 2654212
  135.4 44.4 %collective-permute-start.10 = (bf16[1024,128]{1,0:T(8,128)(2,1)S(1)}, bf16[1024,128]{1,0:T(8,128)(2,1)S(1)}, u32[]{:S(2)}, u32[]{:S(2)}) collective-permute-start(bf16[1024,128]{1,0:T(8,128)(2,1)S(1)} %get-tuple-element.21), channel_id=1, source_target_pairs={{0,1},{1,2},{2,3},{4,5},{5,6},{6,7},{8,9},{9,10},{10,11},{12,13},{... | collective-permute-start | bytes 786440 | tf_op jit(solution)/shard_map/ppermute | solution.py:220
  139.5 40.3 %collective-permute-start.11 = (bf16[1024,128]{1,0:T(8,128)(2,1)S(1)}, bf16[1024,128]{1,0:T(8,128)(2,1)S(1)}, u32[]{:S(2)}, u32[]{:S(2)}) collective-permute-start(bf16[1024,128]{1,0:T(8,128)(2,1)S(1)} %get-tuple-element.20), channel_id=1, source_target_pairs={{1,0},{2,1},{3,2},{5,4},{6,5},{7,6},{9,8},{10,9},{11,10},{13,12},{... | collective-permute-start | bytes 786440 | tf_op jit(solution)/shard_map/ppermute | solution.py:221
  140.8 39.1 %collective-permute-start.8 = (bf16[1024,128]{1,0:T(8,128)(2,1)S(1)}, bf16[1024,128]{1,0:T(8,128)(2,1)}, u32[]{:S(2)}, u32[]{:S(2)}) collective-permute-start(bf16[1024,128]{1,0:T(8,128)(2,1)S(1)} %get-tuple-element.23), channel_id=1, source_target_pairs={{0,4},{4,8},{8,12},{12,16},{16,20},{20,24},{24,28},{1,5},{5,9},{9,... | collective-permute-start | bytes 786440 | tf_op jit(solution)/shard_map/ppermute | solution.py:218
  145.8 34.1 %collective-permute-start.9 = (bf16[1024,128]{1,0:T(8,128)(2,1)S(1)}, bf16[1024,128]{1,0:T(8,128)(2,1)}, u32[]{:S(2)}, u32[]{:S(2)}) collective-permute-start(bf16[1024,128]{1,0:T(8,128)(2,1)S(1)} %get-tuple-element.22), channel_id=1, source_target_pairs={{4,0},{8,4},{12,8},{16,12},{20,16},{24,20},{28,24},{5,1},{9,5},{13... | collective-permute-start | bytes 786440 | tf_op jit(solution)/shard_map/ppermute | solution.py:219
  147.1 12.4 %collective-permute-start.12 = (bf16[32,128]{1,0:T(8,128)(2,1)S(1)}, bf16[32,128]{1,0:T(8,128)(2,1)S(1)}, u32[]{:S(2)}, u32[]{:S(2)}) collective-permute-start(bf16[32,128]{1,0:T(8,128)(2,1)S(1)} %get-tuple-element.19), channel_id=1, source_target_pairs={{0,5},{1,6},{2,7},{4,9},{5,10},{6,11},{8,13},{9,14},{10,15},{12,17... | collective-permute-start | bytes 24584 | tf_op jit(solution)/shard_map/ppermute | solution.py:233
  159.5 5.0 %copy-start.11 = (bf16[32,128]{1,0:T(8,128)(2,1)}, bf16[32,128]{1,0:T(8,128)(2,1)S(1)}, u32[]{:S(2)}) copy-start(bf16[32,128]{1,0:T(8,128)(2,1)S(1)} %collective-permute-done.12.refs_7_) | copy-start | bytes 24580
  159.5 0.7 collective-permute-start.13
  160.2 4.3 %copy-start.13 = (bf16[32,128]{1,0:T(8,128)(2,1)}, bf16[32,128]{1,0:T(8,128)(2,1)S(1)}, u32[]{:S(2)}) copy-start(bf16[32,128]{1,0:T(8,128)(2,1)S(1)} %collective-permute-done.13.refs_8_) | copy-start | bytes 24580
  160.2 0.7 collective-permute-start.14
  160.9 3.6 %copy-start.15 = (bf16[32,128]{1,0:T(8,128)(2,1)}, bf16[32,128]{1,0:T(8,128)(2,1)S(1)}, u32[]{:S(2)}) copy-start(bf16[32,128]{1,0:T(8,128)(2,1)S(1)} %collective-permute-done.14.refs_9_) | copy-start | bytes 24580
  160.9 19.0 %collective-permute-start.15 = (bf16[32,128]{1,0:T(8,128)(2,1)S(1)}, bf16[32,128]{1,0:T(8,128)(2,1)S(1)}, u32[]{:S(2)}, u32[]{:S(2)}) collective-permute-start(bf16[32,128]{1,0:T(8,128)(2,1)S(1)} %get-tuple-element.16), channel_id=1, source_target_pairs={{5,0},{6,1},{7,2},{9,4},{10,5},{11,6},{13,8},{14,9},{15,10},{17,12... | collective-permute-start | bytes 24584 | tf_op jit(solution)/shard_map/ppermute | solution.py:233
  164.5 44.3 %all-to-all-start.1 = ((bf16[8,128,128]{2,1,0:T(8,128)(2,1)}), bf16[8,128,128]{2,1,0:T(8,128)(2,1)S(1)}, u32[]{:S(2)}, u32[]{:S(2)}) async-start(bf16[8,128,128]{2,1,0:T(8,128)(2,1)} %bitcast.16), calls=%async_computation.1 | async-start | bytes 524288 | tf_op jit(solution)/shard_map/all_to_all | solution.py:304
  273.5 2.9 %copy-start.2 = (f32[1024,128]{1,0:T(8,128)S(1)}, f32[1024,128]{1,0:T(8,128)}, u32[]{:S(2)}) copy-start(f32[1024,128]{1,0:T(8,128)} %get-tuple-element.15) | copy-start | bytes 1572868
  (6 other events, 4.2 us)
Sparse Core Ops, SparseCore 0:
  134.3 139.1 all-reduce.2

commit v2 on v1

--- a/solution.py
+++ b/solution.py
@@ -1,3 +1,4 @@
+import functools
 import math
 
 import jax
@@ -21,6 +22,7 @@
 F32 = jnp.float32
 VM = pl.BlockSpec(memory_space=pltpu.VMEM)
 SM = pl.BlockSpec(memory_space=pltpu.SMEM)
+MESH = pl.DeviceIdType.MESH
 LIMIT = 60 * 1024 * 1024
 
 
@@ -72,12 +74,12 @@
     inner = slice(1, 1 + SPAN)
     depth = slice(1, 1 + TILE)
     plane = (SPAN, TILE, EDGE, CH)
-    volume[0, inner, depth] = halo[0][...].astype(F32).reshape(plane)
-    volume[1 + SPAN, inner, depth] = halo[1][...].astype(F32).reshape(plane)
-    volume[inner, 0, depth] = halo[2][...].astype(F32).reshape(plane)
-    volume[inner, 1 + SPAN, depth] = halo[3][...].astype(F32).reshape(plane)
+    volume[0, inner, depth] = halo[0].astype(F32).reshape(plane)
+    volume[1 + SPAN, inner, depth] = halo[1].astype(F32).reshape(plane)
+    volume[inner, 0, depth] = halo[2].astype(F32).reshape(plane)
+    volume[inner, 1 + SPAN, depth] = halo[3].astype(F32).reshape(plane)
     for at, (cx, cy) in enumerate(((0, 0), (0, 1), (1, 0), (1, 1))):
-        line = corners[at][...].astype(F32).reshape(TILE, EDGE, CH)
+        line = corners[at].astype(F32).reshape(TILE, EDGE, CH)
         volume[cx * (1 + SPAN), cy * (1 + SPAN), depth] = line
 
 
@@ -108,7 +110,7 @@
 
 def main_kernel(
     coord, target, feats, mask, halo, corners, returned, weight, down, gather, scatter,
-    sending, grad_out, face_out, conv_out, down_out,
+    sending, grad_out, face_out, sums,
     volume, shifted, columns, faces, conv_acc, grads, back_rows, blocks,
 ):
     fill_volume(volume, halo, corners)
@@ -168,11 +170,14 @@
     lax.fori_loop(0, SLOTS, body, 0)
     face_out[...] = faces[...].reshape(4, FACE, CH).astype(BF)
     for tap in range(27):
-        conv_out[tap * CH : (tap + 1) * CH] = conv_acc[:, tap * CH : (tap + 1) * CH].T
+        sums[tap * CH : (tap + 1) * CH] = conv_acc[:, tap * CH : (tap + 1) * CH].T.astype(BF)
     turned = grads[...].astype(F32).T.astype(BF)
     down_acc = jnp.dot(turned, blocks[...], preferred_element_type=F32)
     for q in range(8):
-        down_out[q * CH : (q + 1) * CH] = down_acc[:, q * CH : (q + 1) * CH].T
+        rows = slice((27 + q) * CH, (28 + q) * CH)
+        sums[rows] = down_acc[:, q * CH : (q + 1) * CH].T.astype(BF)
+    if sums.shape[0] > 35 * CH:
+        sums[35 * CH :] = jnp.zeros((sums.shape[0] - 35 * CH, CH), BF)
 
     def send(s, carry):
         rows = pl.ds(pl.multiple_of(s * 64, 64), 64)
@@ -208,37 +213,225 @@
 FACES = pltpu.VMEM((4, SPAN, TILE, EDGE, CH), F32)
 
 
-def swap_faces(faces):
-    nx, ny = lax.axis_size("gx"), lax.axis_size("gy")
-    up_x = [(i, i + 1) for i in range(nx - 1)]
-    down_x = [(i + 1, i) for i in range(nx - 1)]
-    up_y = [(j, j + 1) for j in range(ny - 1)]
-    down_y = [(j + 1, j) for j in range(ny - 1)]
-    halo = (
-        lax.ppermute(faces[1], "gx", up_x),
-        lax.ppermute(faces[0], "gx", down_x),
-        lax.ppermute(faces[3], "gy", up_y),
-        lax.ppermute(faces[2], "gy", down_y),
-    )
-    corners = []
-    for cx in (0, 1):
-        for cy in (0, 1):
-            line = faces[1 - cx, FACE - SPAN :] if cy == 0 else faces[1 - cx, :SPAN]
-            pairs = [
-                (i * ny + j, (i + 1 - 2 * cx) * ny + j + 1 - 2 * cy)
-                for i in range(nx)
-                for j in range(ny)
-                if 0 <= i + 1 - 2 * cx < nx and 0 <= j + 1 - 2 * cy < ny
-            ]
-            corners.append(lax.ppermute(line, ("gx", "gy"), pairs))
-    return halo, corners
-
-
-def unpack(kernel, at):
-    def wrapped(*refs):
-        kernel(*refs[:at], refs[at : at + 4], refs[at + 4 : at + 8], *refs[at + 8 :])
-
-    return wrapped
+def at_rows(start, size):
+    return pl.ds(pl.multiple_of(start, 16), size)
+
+
+def greet(peers):
+    barrier = pltpu.get_barrier_semaphore()
+    for peer in peers:
+        pl.semaphore_signal(barrier, inc=1, device_id=peer, device_id_type=MESH)
+    pl.semaphore_wait(barrier, len(peers))
+
+
+def around(nx, ny, gx, gy):
+    ring = [
+        (lax.rem(gx + dx + nx, nx), lax.rem(gy + dy + ny, ny))
+        for dx in (-1, 0, 1)
+        for dy in (-1, 0, 1)
+        if dx or dy
+    ]
+    return ring + [(lax.rem(gx + k, nx), gy) for k in range(1, nx)]
+
+
+def border_copies(nx, ny, gx, gy, faces, halo, corners, send, recv):
+    plan = [
+        (1, 0, faces.at[1], halo.at[0]),
+        (-1, 0, faces.at[0], halo.at[1]),
+        (0, 1, faces.at[3], halo.at[2]),
+        (0, -1, faces.at[2], halo.at[3]),
+    ]
+    for at, (cx, cy) in enumerate(((0, 0), (0, 1), (1, 0), (1, 1))):
+        rows = pl.ds(FACE - SPAN if cy == 0 else 0, SPAN)
+        plan.append((1 - 2 * cx, 1 - 2 * cy, faces.at[1 - cx, rows], corners.at[at]))
+    copies = []
+    for at, (dx, dy, source, place) in enumerate(plan):
+        sends = (gx + dx >= 0) & (gx + dx < nx) & (gy + dy >= 0) & (gy + dy < ny)
+        gets = (gx - dx >= 0) & (gx - dx < nx) & (gy - dy >= 0) & (gy - dy < ny)
+        copy = pltpu.make_async_remote_copy(
+            src_ref=source, dst_ref=place, send_sem=send.at[at], recv_sem=recv.at[at],
+            device_id=(lax.rem(gx + dx + nx, nx), lax.rem(gy + dy + ny, ny)),
+            device_id_type=MESH,
+        )
+        copies.append((copy, place, sends, gets))
+    return copies
+
+
+def start_border(copies):
+    for copy, place, sends, gets in copies:
+
+        @pl.when(sends)
+        def _(copy=copy):
+            copy.start()
+
+        @pl.when(jnp.logical_not(gets))
+        def _(place=place):
+            place[...] = jnp.zeros(place.shape, BF)
+
+
+def wait_border(copies):
+    for copy, place, sends, gets in copies:
+
+        @pl.when(sends)
+        def _(copy=copy):
+            copy.wait_send()
+
+        @pl.when(gets)
+        def _(copy=copy):
+            copy.wait_recv()
+
+
+def trade_copies(nx, gx, gy, source, place, send, recv):
+    block = source.shape[0] // nx
+    copies = []
+    for k in range(1, nx):
+        peer = lax.rem(gx + k, nx)
+        copies.append(
+            pltpu.make_async_remote_copy(
+                src_ref=source.at[at_rows(peer * block, block)],
+                dst_ref=place.at[at_rows(gx * block, block)],
+                send_sem=send.at[k - 1], recv_sem=recv.at[k - 1],
+                device_id=(peer, gy), device_id_type=MESH,
+            )
+        )
+    return copies
+
+
+def keep_own(nx, gx, source, place):
+    block = source.shape[0] // nx
+    place[at_rows(gx * block, block)] = source[at_rows(gx * block, block)]
+
+
+def early_kernel(nx, ny, faces, cotangent, halo, corners, returned, send, recv, tsend, trecv):
+    gx, gy = lax.axis_index("gx"), lax.axis_index("gy")
+    greet(around(nx, ny, gx, gy))
+    border = border_copies(nx, ny, gx, gy, faces, halo, corners, send, recv)
+    trade = trade_copies(nx, gx, gy, cotangent, returned, tsend, trecv)
+    start_border(border)
+    for copy in trade:
+        copy.start()
+    keep_own(nx, gx, cotangent, returned)
+    wait_border(border)
+    for copy in trade:
+        copy.wait()
+
+
+def late_kernel(
+    nx, ny, faces, sending, sums, halo, corners, coarse, total,
+    pair_in, line_in, row_in, pair_sum, line_sum, send, recv, tsend, trecv, ssend, srecv,
+):
+    gx, gy = lax.axis_index("gx"), lax.axis_index("gy")
+    core, line, lines = lax.rem(gy, 2), gy // 2, ny // 2
+    half = sums.shape[0] // 2
+    part = half // lines
+    unit = part // nx
+    mate = (gx, gy + 1 - 2 * core)
+    beside = [lax.rem(line + k, lines) for k in range(1, lines)]
+    along = [lax.rem(gx + k, nx) for k in range(1, nx)]
+    greet(around(nx, ny, gx, gy) + [mate] + [(gx, 2 * b + core) for b in beside])
+
+    def copy_to(at, source, place, device):
+        return pltpu.make_async_remote_copy(
+            src_ref=source, dst_ref=place, send_sem=ssend.at[at], recv_sem=srecv.at[at],
+            device_id=device, device_id_type=MESH,
+        )
+
+    def run(copies):
+        for copy in copies:
+            copy.start()
+        for copy in copies:
+            copy.wait()
+
+    border = border_copies(nx, ny, gx, gy, faces, halo, corners, send, recv)
+    trade = trade_copies(nx, gx, gy, sending, coarse, tsend, trecv)
+    first = copy_to(0, sums.at[at_rows((1 - core) * half, half)], pair_in, mate)
+    first.start()
+    start_border(border)
+    for copy in trade:
+        copy.start()
+    keep_own(nx, gx, sending, coarse)
+    first.wait()
+    own = sums[at_rows(core * half, half)].astype(F32)
+    pair_sum[...] = (own + pair_in[...].astype(F32)).astype(BF)
+    run([
+        copy_to(1 + k, pair_sum.at[at_rows(b * part, part)], line_in.at[k], (gx, 2 * b + core))
+        for k, b in enumerate(beside)
+    ])
+    added = pair_sum[at_rows(line * part, part)].astype(F32)
+    for k in range(lines - 1):
+        added = added + line_in[k].astype(F32)
+    line_sum[...] = added.astype(BF)
+    base = lines
+    run([
+        copy_to(base + k, line_sum.at[at_rows(a * unit, unit)], row_in.at[k], (a, gy))
+        for k, a in enumerate(along)
+    ])
+    added = line_sum[at_rows(gx * unit, unit)].astype(F32)
+    for k in range(nx - 1):
+        added = added + row_in[k].astype(F32)
+    start = core * half + line * part
+    mine = at_rows(start + gx * unit, unit)
+    total[mine] = added.astype(BF)
+    base = base + nx - 1
+    run([copy_to(base + k, total.at[mine], total.at[mine], (a, gy)) for k, a in enumerate(along)])
+    base = base + nx - 1
+    mine = at_rows(start, part)
+    run([
+        copy_to(base + k, total.at[mine], total.at[mine], (gx, 2 * b + core))
+        for k, b in enumerate(beside)
+    ])
+    base = base + lines - 1
+    mine = at_rows(core * half, half)
+    run([copy_to(base, total.at[mine], total.at[mine], mate)])
+    wait_border(border)
+    for copy in trade:
+        copy.wait()
+
+
+def swap_early(nx, ny, faces, cotangent):
+    sems = [pltpu.SemaphoreType.DMA((8,))] * 2 + [pltpu.SemaphoreType.DMA((nx - 1,))] * 2
+    return pl.pallas_call(
+        functools.partial(early_kernel, nx, ny),
+        out_shape=(
+            jax.ShapeDtypeStruct((4, FACE, CH), BF),
+            jax.ShapeDtypeStruct((4, SPAN, CH), BF),
+            jax.ShapeDtypeStruct(cotangent.shape, BF),
+        ),
+        in_specs=[VM, VM],
+        out_specs=(VM,) * 3,
+        scratch_shapes=sems,
+        compiler_params=pltpu.CompilerParams(
+            collective_id=0, has_side_effects=True, vmem_limit_bytes=LIMIT
+        ),
+    )(faces, cotangent)
+
+
+def swap_late(nx, ny, faces, sending, sums):
+    rows = sums.shape[0]
+    lines = ny // 2
+    count = 2 * (1 + lines - 1 + nx - 1)
+    sems = [pltpu.SemaphoreType.DMA((8,))] * 2 + [pltpu.SemaphoreType.DMA((nx - 1,))] * 2
+    return pl.pallas_call(
+        functools.partial(late_kernel, nx, ny),
+        out_shape=(
+            jax.ShapeDtypeStruct((4, FACE, CH), BF),
+            jax.ShapeDtypeStruct((4, SPAN, CH), BF),
+            jax.ShapeDtypeStruct(sending.shape, BF),
+            jax.ShapeDtypeStruct(sums.shape, BF),
+        ),
+        in_specs=[VM] * 3,
+        out_specs=(VM,) * 4,
+        scratch_shapes=[
+            pltpu.VMEM((rows // 2, CH), BF),
+            pltpu.VMEM((lines - 1, rows // ny, CH), BF),
+            pltpu.VMEM((nx - 1, rows // (nx * ny), CH), BF),
+            pltpu.VMEM((rows // 2, CH), BF),
+            pltpu.VMEM((rows // ny, CH), BF),
+        ] + sems + [pltpu.SemaphoreType.DMA((count,))] * 2,
+        compiler_params=pltpu.CompilerParams(
+            collective_id=1, has_side_effects=True, vmem_limit_bytes=LIMIT
+        ),
+    )(faces, sending, sums)
 
 
 def per_device(
@@ -267,23 +460,23 @@
         scratch_shapes=[FACES],
         compiler_params=params,
     )(coord, feats, mask)
-    returned = lax.all_to_all(
-        coarse_grad[0, 0].reshape(tiles_x, CAP * quarter, CH),
-        "gx", split_axis=0, concat_axis=0, tiled=True,
-    ).reshape(received, quarter, CH)
-    halo, corners = swap_faces(faces)
+    halo, corners, returned = swap_early(
+        tiles_x, tiles_y, faces, coarse_grad.reshape(received * quarter, CH)
+    )
+    returned = returned.reshape(received, quarter, CH)
+    each = -(-35 * CH // (tiles_x * tiles_y))
+    padded = -(-each // 16) * 16 * tiles_x * tiles_y
     order = pool_order()
-    sending, grad_pre, grad_faces, conv_local, down_local = pl.pallas_call(
-        unpack(main_kernel, 4),
+    sending, grad_pre, grad_faces, sums = pl.pallas_call(
+        main_kernel,
         out_shape=(
             jax.ShapeDtypeStruct((received, quarter, CH), BF),
             jax.ShapeDtypeStruct((SLOTS, VOX, CH), BF),
             jax.ShapeDtypeStruct((4, FACE, CH), BF),
-            jax.ShapeDtypeStruct((27 * CH, CH), F32),
-            jax.ShapeDtypeStruct((8 * CH, CH), F32),
-        ),
-        in_specs=[SM, SM] + [VM] * 15,
-        out_specs=(VM,) * 5,
+            jax.ShapeDtypeStruct((padded, CH), BF),
+        ),
+        in_specs=[SM, SM] + [VM] * 9,
+        out_specs=(VM,) * 4,
         scratch_shapes=[
             VOLUME, SHIFTED, COLUMNS, FACES,
             pltpu.VMEM((CH, 27 * CH), F32),
@@ -296,29 +489,28 @@
             flops=4 * SLOTS * VOX * 27 * CH * CH, bytes_accessed=16 << 20, transcendentals=0
         ),
     )(
-        coord, target, feats, mask, *halo, *corners, returned, conv_weight, down_weight,
+        coord, target, feats, mask, halo, corners, returned, conv_weight, down_weight,
         jnp.asarray(order, BF), jnp.asarray(order.T, BF),
     )
-    conv_sum, down_sum = lax.psum((conv_local, down_local), ("gx", "gy"))
-    grad_halo, grad_corners = swap_faces(grad_faces)
-    coarse = lax.all_to_all(
-        sending.reshape(tiles_x, CAP * quarter, CH), "gx", split_axis=0, concat_axis=0, tiled=True
-    ).reshape(1, 1, received, quarter, CH)
+    grad_halo, grad_corners, coarse, total = swap_late(
+        tiles_x, tiles_y, grad_faces, sending.reshape(received * quarter, CH), sums
+    )
+    coarse = coarse.reshape(1, 1, received, quarter, CH)
     flipped = conv_weight.reshape(27, CH, CH)[::-1].transpose(0, 2, 1).reshape(27 * CH, CH)
     feat_grad = pl.pallas_call(
-        unpack(back_kernel, 3),
+        back_kernel,
         out_shape=jax.ShapeDtypeStruct((SLOTS, VOX, CH), BF),
-        in_specs=[SM] + [VM] * 11,
+        in_specs=[SM] + [VM] * 5,
         out_specs=VM,
         scratch_shapes=[VOLUME, SHIFTED, COLUMNS],
         compiler_params=params,
         cost_estimate=pl.CostEstimate(
             flops=2 * SLOTS * VOX * 27 * CH * CH, bytes_accessed=8 << 20, transcendentals=0
         ),
-    )(coord, grad_pre, mask, *grad_halo, *grad_corners, flipped)
+    )(coord, grad_pre, mask, grad_halo, grad_corners, flipped)
     total_slots = tiles_x * tiles_y * SLOTS
-    conv_grad = conv_sum * (1.0 / math.sqrt(total_slots * VOX))
-    down_grad = down_sum * (1.0 / math.sqrt(total_slots * VOX // 8))
+    conv_grad = total[: 27 * CH].astype(F32) * (1.0 / math.sqrt(total_slots * VOX))
+    down_grad = total[27 * CH : 35 * CH].astype(F32) * (1.0 / math.sqrt(total_slots * VOX // 8))
     return (coarse, feat_grad[None, None], conv_grad, down_grad)
 
 

time: 286 us -> 183 us (0.64)
  waiting for transfers between devices: 87.7 us -> 0 us
  Pallas kernels: 105 us -> 169 us
  starting transfers between devices: 58.8 us -> 0 us
  between operations: 14.4 us -> 0.7 us
  local copies, waits for them, and re-layouts: 12.9 us -> 7.25 us
    psum x1 -> x0, waiting for transfers between devices: 64.7 us -> none  [per_device(): conv_sum, down_sum = lax.psum((conv_local, down_local), ('gx', 'gy'))]
    pallas_call x2 -> x4, Pallas kernels: 101 us -> 165 us  [the longest x1 72 us: per_device(): pl.pallas_call(main_kernel, out_shape=(jax.ShapeDtypeStruct((received, qu...]
    ppermute x16 -> x0, starting transfers between devices: 36.7 us -> none  [the longest x8 16.1 us: swap_faces(): corners.append(lax.ppermute(line, ('gx', 'gy'), pairs))]
    ppermute x16 -> x0, waiting for transfers between devices: 22.9 us -> none  [the longest x8 22.9 us: swap_faces(): corners.append(lax.ppermute(line, ('gx', 'gy'), pairs))]
    all_to_all x2 -> x0, starting transfers between devices: 22.1 us -> none  [the longest x1 15.3 us: per_device(): lax.all_to_all(sending.reshape(tiles_x, CAP * quarter, CH), 'gx', split_a...]
    unnamed x39 -> x11, local copies, waits for them, and re-layouts: 3.64 us -> 0.72 us
  transfers between devices with their start and end apart: 19 -> 0, of which waited for: 4 -> 0; matrix products, arithmetic and copies ran while one was open for 1% -> 0% of each run, Pallas kernels for 10% -> 0%
where the time goes in v2:
time: 183 us; the launch traced here: 181 us
  Pallas kernels  169 us (92%)
  local copies, waits for them, and re-layouts  7.25 us (4%)
  other arithmetic  4.81 us (3%)
    pallas_call x1, Pallas kernels, per_device(): pl.pallas_call(main_kernel, out_shape=(jax.ShapeDtypeStruct((received, qu...  72 us
    pallas_call x1, Pallas kernels, swap_late(): pl.pallas_call(functools.partial(late_kernel, nx, ny), out_shape=(jax.Sha...  41.7 us
    pallas_call x1, Pallas kernels, per_device(): pl.pallas_call(back_kernel, out_shape=jax.ShapeDtypeStruct((SLOTS, VOX, C...  28.1 us
    pallas_call x1, Pallas kernels, swap_early(): pl.pallas_call(functools.partial(early_kernel, nx, ny), out_shape=(jax.Sh...  23.2 us
    pallas_call x1, Pallas kernels, per_device(): pl.pallas_call(face_kernel, out_shape=jax.ShapeDtypeStruct((4, FACE, CH),...  3.73 us

profile of v2, /device:TPU:0, one launch (start us, length us, event | category | flops | bytes accessed | tf_op | source)
XLA Modules:
  0.0 181.4 jit_solution(8898622199177964619)
XLA Ops:
  0.6 0.0 copy-start.3
  0.6 1.3 fusion.1
  2.0 1.3 compare_select_fusion
  3.3 0.8 fusion
  4.1 2.2 %broadcast_in_dim.24.mask = bf16[16,512,128]{2,1,0:T(8,128)(2,1)} broadcast(bf16[16,512]{1,0:T(8,128)(2,1)S(1)} %fusion), dimensions={0,1} | broadcast | bytes 2113536 | tf_op jit(solution)/shard_map/broadcast_in_dim | solution.py:448
  6.3 0.0 copy-done.3
  6.3 0.7 copy.18
  7.0 0.0 copy-start.4
  7.0 3.7 %shard_map.129.faces = bf16[4,1024,128]{2,1,0:T(8,128)(2,1)} custom-call(s32[16,3]{1,0:T(8,128)} %bitcast.26, bf16[16,512,128]{2,1,0:T(8,128)(2,1)} %bitcast.19, bf16[16,512,128]{2,1,0:T(8,128)(2,1)} %broadcast_in_dim.24.mask), custom_call_target="tpu_custom_call" | custom-call | tf_op jit(solution)/shard_map/pallas_call | solution.py:455
  10.8 23.2 %shard_map.130 = (bf16[4,1024,128]{2,1,0:T(8,128)(2,1)}, bf16[4,32,128]{2,1,0:T(8,128)(2,1)}, bf16[1024,128]{1,0:T(8,128)(2,1)}) custom-call(bf16[4,1024,128]{2,1,0:T(8,128)(2,1)} %shard_map.129.faces, bf16[1024,128]{1,0:T(8,128)(2,1)} %bitcast.23), custom_call_target="tpu_custom_call" | custom-call | tf_op jit(solution)/shard_map/pallas_call | solution.py:393
  33.9 0.0 copy-done.4
  34.0 0.5 add_bitcast_fusion.target
  34.5 72.0 %shard_map.131 = (bf16[16,64,128]{2,1,0:T(8,128)(2,1)}, bf16[16,512,128]{2,1,0:T(8,128)(2,1)}, bf16[4,1024,128]{2,1,0:T(8,128)(2,1)}, bf16[4608,128]{1,0:T(8,128)(2,1)}) custom-call(s32[16,3]{1,0:T(8,128)} %bitcast.27, s32[16]{0:T(128)} %add_bitcast_fusion.target, bf16[16,512,128]{2,1,0:T(8,128)(2,1)} %bitcast.20, ...), custom_call_target="tpu_custom_call" | custom-call | flops 14495514624 | bytes 16777216 | tf_op jit(solution)/shard_map/pallas_call | solution.py:470
  106.4 0.0 copy-start.1
  106.4 41.7 %shard_map.132 = (bf16[4,1024,128]{2,1,0:T(8,128)(2,1)}, bf16[4,32,128]{2,1,0:T(8,128)(2,1)}, bf16[1024,128]{1,0:T(8,128)(2,1)}, bf16[4608,128]{1,0:T(8,128)(2,1)}) custom-call(bf16[4,1024,128]{2,1,0:T(8,128)(2,1)} %get-tuple-element.18.faces, bf16[1024,128]{1,0:T(8,128)(2,1)} %bitcast.24, bf16[4608,128]{1,0:T(8,128)(2,1)} %get-tuple-element.20.sums), custom_call_target="tpu_custom_call" | custom-call | tf_op jit(solution)/shard_map/pallas_call | solution.py:414
  148.2 0.0 copy-done.1
  148.2 1.3 copy.16
  149.5 1.0 rev.3
  150.5 0.0 copy-start
  150.5 28.1 %shard_map.133 = bf16[16,512,128]{2,1,0:T(8,128)(2,1)} custom-call(s32[16,3]{1,0:T(8,128)} %bitcast.28, bf16[16,512,128]{2,1,0:T(8,128)(2,1)} %get-tuple-element.22.grad, bf16[16,512,128]{2,1,0:T(8,128)(2,1)} %broadcast_in_dim.24.mask, bf16[4,1024,128]{2,1,0:T(8,128)(2,1)} %get-tuple-element.23.halo, bf16[4,32,128]{2,1,0:T(8,128)(2,1)} %get-tuple-element.24.corners, ...), custom_call_target="tpu_custom_call" | custom-call | flops 7247757312 | bytes 8388608 | tf_op jit(solution)/shard_map/pallas_call | solution.py:500
  178.6 0.0 copy-start.2
  178.6 0.0 copy-done
  178.6 1.3 convert_multiply_fusion
  179.9 0.8 convert_multiply_fusion.1
  180.7 0.0 copy-done.2
  180.7 0.7 copy.20
Async XLA Ops:
  0.6 5.7 %copy-start.3 = (s32[1,1,16,3]{2,1,3,0:T(1,128)S(1)}, s32[1,1,16,3]{2,1,3,0:T(1,128)}, u32[]{:S(2)}) copy-start(s32[1,1,16,3]{2,1,3,0:T(1,128)} %param.12) | copy-start | bytes 580
  7.0 26.9 %copy-start.4 = (s32[1,1,16,2]{2,3,1,0:T(2,128)S(1)}, s32[1,1,16,2]{2,3,1,0:T(2,128)}, u32[]{:S(2)}) copy-start(s32[1,1,16,2]{2,3,1,0:T(2,128)} %param.14) | copy-start | bytes 388
  106.4 41.7 %copy-start.1 = (bf16[3456,128]{1,0:T(8,128)(2,1)S(1)}, bf16[3456,128]{1,0:T(8,128)(2,1)}, u32[]{:S(2)}) copy-start(bf16[3456,128]{1,0:T(8,128)(2,1)} %weight.1) | copy-start | bytes 2654212
  150.5 28.1 %copy-start = (bf16[4608,128]{1,0:T(8,128)(2,1)S(1)}, bf16[4608,128]{1,0:T(8,128)(2,1)}, u32[]{:S(2)}) copy-start(bf16[4608,128]{1,0:T(8,128)(2,1)} %get-tuple-element.25) | copy-start | bytes 3538948
  178.6 2.2 %copy-start.2 = (bf16[1024,128]{1,0:T(8,128)(2,1)S(1)}, bf16[1024,128]{1,0:T(8,128)(2,1)}, u32[]{:S(2)}) copy-start(bf16[1024,128]{1,0:T(8,128)(2,1)} %get-tuple-element.21) | copy-start | bytes 786436

commit v3 on v2

--- a/solution.py
+++ b/solution.py
@@ -3,7 +3,6 @@
 
 import jax
 import jax.numpy as jnp
-import numpy as np
 from jax import lax
 from jax.experimental import pallas as pl
 from jax.experimental.pallas import tpu as pltpu
@@ -26,13 +25,35 @@
 LIMIT = 60 * 1024 * 1024
 
 
-def pool_order():
-    order = (
-        np.arange(VOX).reshape(4, 2, 4, 2, 4, 2).transpose(1, 3, 5, 0, 2, 4).reshape(-1)
+def half_rows(first, second):
+    low = lax.broadcasted_iota(jnp.int32, first.shape, 1) < 4
+    return (
+        jnp.where(low, first, pltpu.roll(second, 4, 1)),
+        jnp.where(low, pltpu.roll(first, 4, 1), second),
     )
-    matrix = np.zeros((VOX, VOX), np.float32)
-    matrix[np.arange(VOX), order] = 1.0
-    return matrix
+
+
+def pool_rows(voxels):
+    found = [None] * 8
+    for pz in range(2):
+        lines = voxels[pl.ds(pz, VOX // 2, stride=2), :].reshape(4, 2, 4, EDGE, CH)
+        for px in range(2):
+            pair = lines[:, px].reshape(EDGE, 2, EDGE, CH)
+            for py, part in enumerate(half_rows(pair[:, 0], pair[:, 1])):
+                found[4 * px + 2 * py + pz] = part.reshape(64, CH)
+    return found
+
+
+def unpool_rows(parts, voxels):
+    for pz in range(2):
+        planes = []
+        for px in range(2):
+            first = parts[4 * px + pz].reshape(EDGE, EDGE, CH)
+            second = parts[4 * px + 2 + pz].reshape(EDGE, EDGE, CH)
+            pair = jnp.stack(half_rows(first, second), axis=1)
+            planes.append(pair.reshape(4, 4, EDGE, CH))
+        lines = jnp.stack(planes, axis=1).reshape(VOX // 2, CH)
+        voxels[pl.ds(pz, VOX // 2, stride=2), :] = lines
 
 
 def put_faces(faces, cube, x, y, z):
@@ -53,8 +74,20 @@
         faces[3, pl.ds(x * EDGE, EDGE), z] = cube[:, EDGE - 1]
 
 
-def face_kernel(coord, feats, mask, out, faces):
+def face_kernel(coord, count, feats, voxel_mask, out, mask, faces, turned):
     faces[...] = jnp.zeros_like(faces)
+    slot = lax.broadcasted_iota(jnp.int32, (SLOTS, VOX), 0)
+    filled = slot < jnp.where(slot < BORDER, count[0], count[1] + BORDER)
+    turned[...] = jnp.where(filled, voxel_mask[...], 0).astype(F32).T.astype(BF)
+
+    def widen(s, carry):
+        pick = lax.broadcasted_iota(jnp.int32, (SLOTS, CH), 0) == s
+        mask[s] = jnp.dot(
+            turned[...], pick.astype(F32).astype(BF), preferred_element_type=F32
+        ).astype(BF)
+        return carry
+
+    lax.fori_loop(0, SLOTS, widen, 0)
 
     def body(s, carry):
         cube = (feats[s].astype(F32) * mask[s].astype(F32)).reshape(EDGE, EDGE, EDGE, CH)
@@ -109,9 +142,10 @@
 
 
 def main_kernel(
-    coord, target, feats, mask, halo, corners, returned, weight, down, gather, scatter,
+    coord, target, feats, mask, halo, corners, returned, weight, down,
     sending, grad_out, face_out, sums,
-    volume, shifted, columns, faces, conv_acc, grads, back_rows, blocks,
+    volume, shifted_a, columns_a, shifted_b, columns_b, faces, conv_acc, grads, back_rows,
+    blocks, voxels_a, voxels_b,
 ):
     fill_volume(volume, halo, corners)
     faces[...] = jnp.zeros_like(faces)
@@ -136,48 +170,48 @@
 
     lax.fori_loop(0, SLOTS // 4, spread, 0)
 
-    def body(s, carry):
-        x, y, z = coord[s, 0], coord[s, 1], coord[s, 2]
+    def local(s, columns, voxels):
         rows = pl.ds(pl.multiple_of(s * 64, 64), 64)
-        unfold(volume, shifted, columns, x, y, z)
         preact = jnp.dot(columns[...], weight[...], preferred_element_type=F32)
         active = mask[s].astype(F32)
         sig = jax.nn.sigmoid(preact)
-        activated = (preact * sig * active).astype(BF)
-        ordered = jnp.dot(gather[...], activated, preferred_element_type=F32).astype(BF)
-        blocks[rows] = jnp.concatenate([ordered[64 * q : 64 * q + 64] for q in range(8)], axis=1)
+        voxels[...] = preact * sig * active
+        blocks[rows] = jnp.concatenate([p.astype(BF) for p in pool_rows(voxels)], axis=1)
         wide = back_rows[rows]
-        tall = jnp.concatenate([wide[:, CH * q : CH * q + CH] for q in range(8)], axis=0)
-        head = tall.astype(BF)
-        rest = (tall - head.astype(F32)).astype(BF)
-        both = jnp.dot(
-            scatter[...], jnp.concatenate([head, rest], axis=1), preferred_element_type=F32
+        unpool_rows([wide[:, CH * q : CH * q + CH] for q in range(8)], voxels)
+        grad = (voxels[...] * active * sig * (1.0 + preact * (1.0 - sig))).astype(BF)
+        grad_out[s] = grad
+        return grad.astype(F32).T.astype(BF)
+
+    def body(i, carry):
+        s, t = 2 * i, 2 * i + 1
+        unfold(volume, shifted_a, columns_a, coord[s, 0], coord[s, 1], coord[s, 2])
+        unfold(volume, shifted_b, columns_b, coord[t, 0], coord[t, 1], coord[t, 2])
+        first = local(s, columns_a, voxels_a)
+        second = local(t, columns_b, voxels_b)
+        conv_acc[...] += jnp.dot(first, columns_a[...], preferred_element_type=F32) + jnp.dot(
+            second, columns_b[...], preferred_element_type=F32
         )
-        grad_act = both[:, :CH] + both[:, CH:]
-        grad_f32 = grad_act * active * sig * (1.0 + preact * (1.0 - sig))
-        grad = grad_f32.astype(BF)
-        grad_out[s] = grad
-        rounded = grad.astype(F32)
-
-        @pl.when(s < BORDER)
-        def _():
-            put_faces(faces, rounded.reshape(EDGE, EDGE, EDGE, CH), x, y, z)
-
-        turned = rounded.T.astype(BF)
-        conv_acc[...] += jnp.dot(turned, columns[...], preferred_element_type=F32)
-        return carry
-
-    lax.fori_loop(0, SLOTS, body, 0)
+        return carry
+
+    lax.fori_loop(0, SLOTS // 2, body, 0)
+
+    def edge(s, carry):
+        cube = grad_out[s].astype(F32).reshape(EDGE, EDGE, EDGE, CH)
+        put_faces(faces, cube, coord[s, 0], coord[s, 1], coord[s, 2])
+        return carry
+
+    lax.fori_loop(0, BORDER, edge, 0)
     face_out[...] = faces[...].reshape(4, FACE, CH).astype(BF)
     for tap in range(27):
-        sums[tap * CH : (tap + 1) * CH] = conv_acc[:, tap * CH : (tap + 1) * CH].T.astype(BF)
+        sums[tap * CH : (tap + 1) * CH] = conv_acc[:, tap * CH : (tap + 1) * CH].T
     turned = grads[...].astype(F32).T.astype(BF)
     down_acc = jnp.dot(turned, blocks[...], preferred_element_type=F32)
     for q in range(8):
         rows = slice((27 + q) * CH, (28 + q) * CH)
-        sums[rows] = down_acc[:, q * CH : (q + 1) * CH].T.astype(BF)
+        sums[rows] = down_acc[:, q * CH : (q + 1) * CH].T
     if sums.shape[0] > 35 * CH:
-        sums[35 * CH :] = jnp.zeros((sums.shape[0] - 35 * CH, CH), BF)
+        sums[35 * CH :] = jnp.zeros((sums.shape[0] - 35 * CH, CH), F32)
 
     def send(s, carry):
         rows = pl.ds(pl.multiple_of(s * 64, 64), 64)
@@ -188,8 +222,14 @@
     lax.fori_loop(0, SLOTS, send, 0)
 
 
-def back_kernel(coord, grad, mask, halo, corners, weight, out, volume, shifted, columns):
+def back_kernel(
+    coord, grad, mask, halo, corners, weight, out,
+    volume, shifted_a, columns_a, shifted_b, columns_b, flipped,
+):
     fill_volume(volume, halo, corners)
+    for tap in range(27):
+        block = weight[(26 - tap) * CH : (27 - tap) * CH].astype(F32)
+        flipped[tap * CH : (tap + 1) * CH] = block.T.astype(BF)
 
     def place(s, carry):
         cube = grad[s].astype(F32).reshape(EDGE, EDGE, EDGE, CH)
@@ -198,18 +238,22 @@
 
     lax.fori_loop(0, SLOTS, place, 0)
 
-    def body(s, carry):
-        unfold(volume, shifted, columns, coord[s, 0], coord[s, 1], coord[s, 2])
-        back = jnp.dot(columns[...], weight[...], preferred_element_type=F32)
-        out[s] = (back * mask[s].astype(F32)).astype(BF)
-        return carry
-
-    lax.fori_loop(0, SLOTS, body, 0)
+    def body(i, carry):
+        s, t = 2 * i, 2 * i + 1
+        unfold(volume, shifted_a, columns_a, coord[s, 0], coord[s, 1], coord[s, 2])
+        unfold(volume, shifted_b, columns_b, coord[t, 0], coord[t, 1], coord[t, 2])
+        for slot, columns in ((s, columns_a), (t, columns_b)):
+            back = jnp.dot(columns[...], flipped[...], preferred_element_type=F32)
+            out[slot] = (back * mask[slot].astype(F32)).astype(BF)
+        return carry
+
+    lax.fori_loop(0, SLOTS // 2, body, 0)
 
 
 VOLUME = pltpu.VMEM((SPAN + 2, SPAN + 2, TILE + 2, EDGE, CH), F32)
 SHIFTED = pltpu.VMEM((3, EDGE + 2, EDGE + 2, EDGE, CH), F32)
 COLUMNS = pltpu.VMEM((VOX, 27 * CH), BF)
+PAIR = [SHIFTED, COLUMNS, SHIFTED, COLUMNS]
 FACES = pltpu.VMEM((4, SPAN, TILE, EDGE, CH), F32)
 
 
@@ -318,7 +362,7 @@
 
 def late_kernel(
     nx, ny, faces, sending, sums, halo, corners, coarse, total,
-    pair_in, line_in, row_in, pair_sum, line_sum, send, recv, tsend, trecv, ssend, srecv,
+    pair_in, line_in, row_in, pair_out, pair_sum, pair_send, line_sum, line_send, send, recv, tsend, trecv, ssend, srecv,
 ):
     gx, gy = lax.axis_index("gx"), lax.axis_index("gy")
     core, line, lines = lax.rem(gy, 2), gy // 2, ny // 2
@@ -344,29 +388,31 @@
 
     border = border_copies(nx, ny, gx, gy, faces, halo, corners, send, recv)
     trade = trade_copies(nx, gx, gy, sending, coarse, tsend, trecv)
-    first = copy_to(0, sums.at[at_rows((1 - core) * half, half)], pair_in, mate)
+    pair_out[...] = sums[at_rows((1 - core) * half, half)].astype(BF)
+    first = copy_to(0, pair_out, pair_in, mate)
     first.start()
     start_border(border)
     for copy in trade:
         copy.start()
     keep_own(nx, gx, sending, coarse)
     first.wait()
-    own = sums[at_rows(core * half, half)].astype(F32)
-    pair_sum[...] = (own + pair_in[...].astype(F32)).astype(BF)
+    pair_sum[...] = sums[at_rows(core * half, half)] + pair_in[...].astype(F32)
+    pair_send[...] = pair_sum[...].astype(BF)
     run([
-        copy_to(1 + k, pair_sum.at[at_rows(b * part, part)], line_in.at[k], (gx, 2 * b + core))
+        copy_to(1 + k, pair_send.at[at_rows(b * part, part)], line_in.at[k], (gx, 2 * b + core))
         for k, b in enumerate(beside)
     ])
-    added = pair_sum[at_rows(line * part, part)].astype(F32)
+    added = pair_sum[at_rows(line * part, part)]
     for k in range(lines - 1):
         added = added + line_in[k].astype(F32)
-    line_sum[...] = added.astype(BF)
+    line_sum[...] = added
+    line_send[...] = added.astype(BF)
     base = lines
     run([
-        copy_to(base + k, line_sum.at[at_rows(a * unit, unit)], row_in.at[k], (a, gy))
+        copy_to(base + k, line_send.at[at_rows(a * unit, unit)], row_in.at[k], (a, gy))
         for k, a in enumerate(along)
     ])
-    added = line_sum[at_rows(gx * unit, unit)].astype(F32)
+    added = line_sum[at_rows(gx * unit, unit)]
     for k in range(nx - 1):
         added = added + row_in[k].astype(F32)
     start = core * half + line * part
@@ -426,6 +472,9 @@
             pltpu.VMEM((lines - 1, rows // ny, CH), BF),
             pltpu.VMEM((nx - 1, rows // (nx * ny), CH), BF),
             pltpu.VMEM((rows // 2, CH), BF),
+            pltpu.VMEM((rows // 2, CH), F32),
+            pltpu.VMEM((rows // 2, CH), BF),
+            pltpu.VMEM((rows // ny, CH), F32),
             pltpu.VMEM((rows // ny, CH), BF),
         ] + sems + [pltpu.SemaphoreType.DMA((count,))] * 2,
         compiler_params=pltpu.CompilerParams(
@@ -442,47 +491,45 @@
     quarter = VOX // 8
     received = CAP * tiles_x
     params = pltpu.CompilerParams(vmem_limit_bytes=LIMIT)
-    slot_ids = jnp.arange(SLOTS, dtype=jnp.int32)
-    counts = brick_count[0, 0]
-    occupied = jnp.where(slot_ids < BORDER, slot_ids < counts[0], slot_ids - BORDER < counts[1])
-    mask = jnp.broadcast_to(
-        jnp.where(occupied[:, None], voxel_mask[0, 0], 0).astype(BF)[:, :, None], (SLOTS, VOX, CH)
-    )
     coord = brick_coord[0, 0]
     target = route[0, 0, :, 0] * CAP + route[0, 0, :, 1]
     feats = feats[0, 0]
 
-    faces = pl.pallas_call(
+    faces, mask = pl.pallas_call(
         face_kernel,
-        out_shape=jax.ShapeDtypeStruct((4, FACE, CH), BF),
-        in_specs=[SM, VM, VM],
-        out_specs=VM,
-        scratch_shapes=[FACES],
+        out_shape=(
+            jax.ShapeDtypeStruct((4, FACE, CH), BF),
+            jax.ShapeDtypeStruct((SLOTS, VOX, CH), BF),
+        ),
+        in_specs=[SM, SM, VM, VM],
+        out_specs=(VM, VM),
+        scratch_shapes=[FACES, pltpu.VMEM((VOX, SLOTS), BF)],
         compiler_params=params,
-    )(coord, feats, mask)
+    )(coord, brick_count[0, 0], feats, voxel_mask[0, 0])
     halo, corners, returned = swap_early(
         tiles_x, tiles_y, faces, coarse_grad.reshape(received * quarter, CH)
     )
     returned = returned.reshape(received, quarter, CH)
     each = -(-35 * CH // (tiles_x * tiles_y))
     padded = -(-each // 16) * 16 * tiles_x * tiles_y
-    order = pool_order()
     sending, grad_pre, grad_faces, sums = pl.pallas_call(
         main_kernel,
         out_shape=(
             jax.ShapeDtypeStruct((received, quarter, CH), BF),
             jax.ShapeDtypeStruct((SLOTS, VOX, CH), BF),
             jax.ShapeDtypeStruct((4, FACE, CH), BF),
-            jax.ShapeDtypeStruct((padded, CH), BF),
-        ),
-        in_specs=[SM, SM] + [VM] * 9,
+            jax.ShapeDtypeStruct((padded, CH), F32),
+        ),
+        in_specs=[SM, SM] + [VM] * 7,
         out_specs=(VM,) * 4,
         scratch_shapes=[
-            VOLUME, SHIFTED, COLUMNS, FACES,
+            VOLUME, *PAIR, FACES,
             pltpu.VMEM((CH, 27 * CH), F32),
             pltpu.VMEM((SLOTS * quarter, CH), BF),
             pltpu.VMEM((SLOTS * quarter, 8 * CH), F32),
             pltpu.VMEM((SLOTS * quarter, 8 * CH), BF),
+            pltpu.VMEM((VOX, CH), F32),
+            pltpu.VMEM((VOX, CH), F32),
         ],
         compiler_params=params,
         cost_estimate=pl.CostEstimate(
@@ -490,24 +537,22 @@
         ),
     )(
         coord, target, feats, mask, halo, corners, returned, conv_weight, down_weight,
-        jnp.asarray(order, BF), jnp.asarray(order.T, BF),
     )
     grad_halo, grad_corners, coarse, total = swap_late(
         tiles_x, tiles_y, grad_faces, sending.reshape(received * quarter, CH), sums
     )
     coarse = coarse.reshape(1, 1, received, quarter, CH)
-    flipped = conv_weight.reshape(27, CH, CH)[::-1].transpose(0, 2, 1).reshape(27 * CH, CH)
     feat_grad = pl.pallas_call(
         back_kernel,
         out_shape=jax.ShapeDtypeStruct((SLOTS, VOX, CH), BF),
         in_specs=[SM] + [VM] * 5,
         out_specs=VM,
-        scratch_shapes=[VOLUME, SHIFTED, COLUMNS],
+        scratch_shapes=[VOLUME, *PAIR, pltpu.VMEM((27 * CH, CH), BF)],
         compiler_params=params,
         cost_estimate=pl.CostEstimate(
             flops=2 * SLOTS * VOX * 27 * CH * CH, bytes_accessed=8 << 20, transcendentals=0
         ),
-    )(coord, grad_pre, mask, grad_halo, grad_corners, flipped)
+    )(coord, grad_pre, mask, grad_halo, grad_corners, conv_weight)
     total_slots = tiles_x * tiles_y * SLOTS
     conv_grad = total[: 27 * CH].astype(F32) * (1.0 / math.sqrt(total_slots * VOX))
     down_grad = total[27 * CH : 35 * CH].astype(F32) * (1.0 / math.sqrt(total_slots * VOX // 8))

time: 183 us -> 152 us (0.83)
  Pallas kernels: 169 us -> 143 us
  local copies, waits for them, and re-layouts: 7.25 us -> 2.06 us
    pallas_call x1, Pallas kernels: 72 us -> 44.8 us  [per_device(): pl.pallas_call(main_kernel, out_shape=(jax.ShapeDtypeStruct((received, qu...]
    pallas_call x1, Pallas kernels: 3.73 us -> 6.26 us  [per_device(): pl.pallas_call(face_kernel, out_shape=(jax.ShapeDtypeStruct((4, FACE, CH)...]
    broadcast_in_dim x1 -> x0, local copies, waits for them, and re-layouts: 2.25 us -> none  [per_device(): jnp.broadcast_to(jnp.where(occupied[:, None], voxel_mask[0, 0], 0).astype...]
where the time goes in v3:
time: 152 us; the launch traced here: 150 us
  Pallas kernels  143 us (94%)
  other arithmetic  3.43 us (2%)
  local copies, waits for them, and re-layouts  2.06 us (1%)
    pallas_call x1, Pallas kernels, per_device(): pl.pallas_call(main_kernel, out_shape=(jax.ShapeDtypeStruct((received, qu...  44.8 us
    pallas_call x1, Pallas kernels, swap_late(): pl.pallas_call(functools.partial(late_kernel, nx, ny), out_shape=(jax.Sha...  42 us
    pallas_call x1, Pallas kernels, per_device(): pl.pallas_call(back_kernel, out_shape=jax.ShapeDtypeStruct((SLOTS, VOX, C...  27.3 us
    pallas_call x1, Pallas kernels, swap_early(): pl.pallas_call(functools.partial(early_kernel, nx, ny), out_shape=(jax.Sh...  23.1 us
    pallas_call x1, Pallas kernels, per_device(): pl.pallas_call(face_kernel, out_shape=(jax.ShapeDtypeStruct((4, FACE, CH)...  6.26 us

profile of v3, /device:TPU:0, one launch (start us, length us, event | category | flops | bytes accessed | tf_op | source)
XLA Modules:
  0.0 149.6 jit_solution(2745810411250250799)
XLA Ops:
  0.6 1.3 add_bitcast_fusion.target
  1.9 1.4 copy.15
  3.3 6.3 %shard_map.111 = (bf16[4,1024,128]{2,1,0:T(8,128)(2,1)}, bf16[16,512,128]{2,1,0:T(8,128)(2,1)}) custom-call(s32[16,3]{1,0:T(8,128)} %bitcast.17, s32[2]{0:T(128)} %bitcast.20, bf16[16,512,128]{2,1,0:T(8,128)(2,1)} %bitcast.11, s32[16,512]{1,0:T(8,128)} %bitcast.16), custom_call_target="tpu_custom_call" | custom-call | tf_op jit(solution)/shard_map/pallas_call | solution.py:498
  9.5 23.1 %shard_map.112 = (bf16[4,1024,128]{2,1,0:T(8,128)(2,1)}, bf16[4,32,128]{2,1,0:T(8,128)(2,1)}, bf16[1024,128]{1,0:T(8,128)(2,1)}) custom-call(bf16[4,1024,128]{2,1,0:T(8,128)(2,1)} %get-tuple-element.18.faces, bf16[1024,128]{1,0:T(8,128)(2,1)} %bitcast.14), custom_call_target="tpu_custom_call" | custom-call | tf_op jit(solution)/shard_map/pallas_call | solution.py:439
  32.7 44.8 %shard_map.113 = (bf16[16,64,128]{2,1,0:T(8,128)(2,1)}, bf16[16,512,128]{2,1,0:T(8,128)(2,1)}, bf16[4,1024,128]{2,1,0:T(8,128)(2,1)}, f32[4608,128]{1,0:T(8,128)}) custom-call(s32[16,3]{1,0:T(8,128)} %bitcast.18, s32[16]{0:T(128)} %add_bitcast_fusion.target, bf16[16,512,128]{2,1,0:T(8,128)(2,1)} %bitcast.12, bf16[16,512,128]{2,1,0:T(8,128)(2,1)} %get-tuple-element.17.mask, ...), custom_call_target="tpu_custom_call" | custom-call | flops 14495514624 | bytes 16777216 | tf_op jit(solution)/shard_map/pallas_call | solution.py:515
  77.4 42.0 %shard_map.114 = (bf16[4,1024,128]{2,1,0:T(8,128)(2,1)}, bf16[4,32,128]{2,1,0:T(8,128)(2,1)}, bf16[1024,128]{1,0:T(8,128)(2,1)}, bf16[4608,128]{1,0:T(8,128)(2,1)}) custom-call(bf16[4,1024,128]{2,1,0:T(8,128)(2,1)} %get-tuple-element.22.faces, bf16[1024,128]{1,0:T(8,128)(2,1)} %bitcast.13, f32[4608,128]{1,0:T(8,128)} %get-tuple-element.24.sums), custom_call_target="tpu_custom_call" | custom-call | tf_op jit(solution)/shard_map/pallas_call | solution.py:460
  119.4 0.0 copy-start
  119.5 27.3 %shard_map.115 = bf16[16,512,128]{2,1,0:T(8,128)(2,1)} custom-call(s32[16,3]{1,0:T(8,128)} %bitcast.19, bf16[16,512,128]{2,1,0:T(8,128)(2,1)} %get-tuple-element.26.grad, bf16[16,512,128]{2,1,0:T(8,128)(2,1)} %get-tuple-element.17.mask, bf16[4,1024,128]{2,1,0:T(8,128)(2,1)} %get-tuple-element.27.halo, bf16[4,32,128]{2,1,0:T(8,128)(2,1)} %get-tuple-element.28.corners, ...), custom_call_target="tpu_custom_call" | custom-call | flops 7247757312 | bytes 8388608 | tf_op jit(solution)/shard_map/pallas_call | solution.py:545
  146.7 0.0 copy-start.1
  146.7 0.0 copy-done
  146.7 0.8 convert_multiply_fusion.1
  147.6 1.3 convert_multiply_fusion
  148.9 0.0 copy-done.1
  148.9 0.7 copy.17
Async XLA Ops:
  119.4 27.3 %copy-start = (bf16[4608,128]{1,0:T(8,128)(2,1)S(1)}, bf16[4608,128]{1,0:T(8,128)(2,1)}, u32[]{:S(2)}) copy-start(bf16[4608,128]{1,0:T(8,128)(2,1)} %get-tuple-element.29) | copy-start | bytes 3538948
  146.7 2.2 %copy-start.1 = (bf16[1024,128]{1,0:T(8,128)(2,1)S(1)}, bf16[1024,128]{1,0:T(8,128)(2,1)}, u32[]{:S(2)}) copy-start(bf16[1024,128]{1,0:T(8,128)(2,1)} %get-tuple-element.25) | copy-start | bytes 786436

commit v4 on v3

--- a/solution.py
+++ b/solution.py
@@ -419,16 +419,32 @@
     mine = at_rows(start + gx * unit, unit)
     total[mine] = added.astype(BF)
     base = base + nx - 1
-    run([copy_to(base + k, total.at[mine], total.at[mine], (a, gy)) for k, a in enumerate(along)])
+    spread = [copy_to(base + k, total.at[mine], total.at[mine], (a, gy)) for k, a in enumerate(along)]
+    for copy in spread:
+        copy.start()
     base = base + nx - 1
-    mine = at_rows(start, part)
-    run([
-        copy_to(base + k, total.at[mine], total.at[mine], (gx, 2 * b + core))
-        for k, b in enumerate(beside)
-    ])
-    base = base + lines - 1
-    mine = at_rows(core * half, half)
-    run([copy_to(base, total.at[mine], total.at[mine], mate)])
+    across = []
+    for step in range(nx):
+        if step:
+            spread[step - 1].wait_recv()
+        rows = at_rows(start + lax.rem(gx - step + nx, nx) * unit, unit)
+        for b in beside:
+            at = base + len(across)
+            across.append(copy_to(at, total.at[rows], total.at[rows], (gx, 2 * b + core)))
+            across[-1].start()
+    base = base + nx * (lines - 1)
+    last = []
+    for k in range(lines):
+        if k:
+            for step in range(nx):
+                across[step * (lines - 1) + k - 1].wait_recv()
+        rows = at_rows(core * half + lax.rem(line - k + lines, lines) * part, part)
+        last.append(copy_to(base + k, total.at[rows], total.at[rows], mate))
+        last[-1].start()
+    for copy in spread + across:
+        copy.wait_send()
+    for copy in last:
+        copy.wait()
     wait_border(border)
     for copy in trade:
         copy.wait()
@@ -455,7 +471,7 @@
 def swap_late(nx, ny, faces, sending, sums):
     rows = sums.shape[0]
     lines = ny // 2
-    count = 2 * (1 + lines - 1 + nx - 1)
+    count = 2 * (lines + nx - 1) + nx * (lines - 1)
     sems = [pltpu.SemaphoreType.DMA((8,))] * 2 + [pltpu.SemaphoreType.DMA((nx - 1,))] * 2
     return pl.pallas_call(
         functools.partial(late_kernel, nx, ny),

time: 152 us -> 149 us (0.980); the launches traced: 150 us -> 149 us
  no operation moved by 1% of the time
where the time goes in v4:
time: 149 us
  Pallas kernels  142 us (95%)
  other arithmetic  3.43 us (2%)
  local copies, waits for them, and re-layouts  2.06 us (1%)
    pallas_call x1, Pallas kernels, per_device(): pl.pallas_call(main_kernel, out_shape=(jax.ShapeDtypeStruct((received, qu...  44.8 us
    pallas_call x1, Pallas kernels, swap_late(): pl.pallas_call(functools.partial(late_kernel, nx, ny), out_shape=(jax.Sha...  40.9 us
    pallas_call x1, Pallas kernels, per_device(): pl.pallas_call(back_kernel, out_shape=jax.ShapeDtypeStruct((SLOTS, VOX, C...  27.3 us
    pallas_call x1, Pallas kernels, swap_early(): pl.pallas_call(functools.partial(early_kernel, nx, ny), out_shape=(jax.Sh...  23.1 us
    pallas_call x1, Pallas kernels, per_device(): pl.pallas_call(face_kernel, out_shape=(jax.ShapeDtypeStruct((4, FACE, CH)...  6.26 us

profile of v4, /device:TPU:0, one launch (start us, length us, event | category | flops | bytes accessed | tf_op | source)
XLA Modules:
  0.0 148.6 jit_solution(15681964266351106614)
XLA Ops:
  0.6 1.3 add_bitcast_fusion.target
  1.9 1.4 copy.15
  3.3 6.3 %shard_map.111 = (bf16[4,1024,128]{2,1,0:T(8,128)(2,1)}, bf16[16,512,128]{2,1,0:T(8,128)(2,1)}) custom-call(s32[16,3]{1,0:T(8,128)} %bitcast.17, s32[2]{0:T(128)} %bitcast.20, bf16[16,512,128]{2,1,0:T(8,128)(2,1)} %bitcast.11, s32[16,512]{1,0:T(8,128)} %bitcast.16), custom_call_target="tpu_custom_call" | custom-call | tf_op jit(solution)/shard_map/pallas_call | solution.py:514
  9.5 23.1 %shard_map.112 = (bf16[4,1024,128]{2,1,0:T(8,128)(2,1)}, bf16[4,32,128]{2,1,0:T(8,128)(2,1)}, bf16[1024,128]{1,0:T(8,128)(2,1)}) custom-call(bf16[4,1024,128]{2,1,0:T(8,128)(2,1)} %get-tuple-element.18.faces, bf16[1024,128]{1,0:T(8,128)(2,1)} %bitcast.14), custom_call_target="tpu_custom_call" | custom-call | tf_op jit(solution)/shard_map/pallas_call | solution.py:455
  32.7 44.8 %shard_map.113 = (bf16[16,64,128]{2,1,0:T(8,128)(2,1)}, bf16[16,512,128]{2,1,0:T(8,128)(2,1)}, bf16[4,1024,128]{2,1,0:T(8,128)(2,1)}, f32[4608,128]{1,0:T(8,128)}) custom-call(s32[16,3]{1,0:T(8,128)} %bitcast.18, s32[16]{0:T(128)} %add_bitcast_fusion.target, bf16[16,512,128]{2,1,0:T(8,128)(2,1)} %bitcast.12, bf16[16,512,128]{2,1,0:T(8,128)(2,1)} %get-tuple-element.17.mask, ...), custom_call_target="tpu_custom_call" | custom-call | flops 14495514624 | bytes 16777216 | tf_op jit(solution)/shard_map/pallas_call | solution.py:531
  77.4 40.9 %shard_map.114 = (bf16[4,1024,128]{2,1,0:T(8,128)(2,1)}, bf16[4,32,128]{2,1,0:T(8,128)(2,1)}, bf16[1024,128]{1,0:T(8,128)(2,1)}, bf16[4608,128]{1,0:T(8,128)(2,1)}) custom-call(bf16[4,1024,128]{2,1,0:T(8,128)(2,1)} %get-tuple-element.22.faces, bf16[1024,128]{1,0:T(8,128)(2,1)} %bitcast.13, f32[4608,128]{1,0:T(8,128)} %get-tuple-element.24.sums), custom_call_target="tpu_custom_call" | custom-call | tf_op jit(solution)/shard_map/pallas_call | solution.py:476
  118.4 0.0 copy-start
  118.4 27.3 %shard_map.115 = bf16[16,512,128]{2,1,0:T(8,128)(2,1)} custom-call(s32[16,3]{1,0:T(8,128)} %bitcast.19, bf16[16,512,128]{2,1,0:T(8,128)(2,1)} %get-tuple-element.26.grad, bf16[16,512,128]{2,1,0:T(8,128)(2,1)} %get-tuple-element.17.mask, bf16[4,1024,128]{2,1,0:T(8,128)(2,1)} %get-tuple-element.27.halo, bf16[4,32,128]{2,1,0:T(8,128)(2,1)} %get-tuple-element.28.corners, ...), custom_call_target="tpu_custom_call" | custom-call | flops 7247757312 | bytes 8388608 | tf_op jit(solution)/shard_map/pallas_call | solution.py:561
  145.7 0.0 copy-start.1
  145.7 0.0 copy-done
  145.7 0.8 convert_multiply_fusion.1
  146.5 1.3 convert_multiply_fusion
  147.8 0.0 copy-done.1
  147.8 0.7 copy.17
Async XLA Ops:
  118.4 27.3 %copy-start = (bf16[4608,128]{1,0:T(8,128)(2,1)S(1)}, bf16[4608,128]{1,0:T(8,128)(2,1)}, u32[]{:S(2)}) copy-start(bf16[4608,128]{1,0:T(8,128)(2,1)} %get-tuple-element.29) | copy-start | bytes 3538948
  145.7 2.2 %copy-start.1 = (bf16[1024,128]{1,0:T(8,128)(2,1)S(1)}, bf16[1024,128]{1,0:T(8,128)(2,1)}, u32[]{:S(2)}) copy-start(bf16[1024,128]{1,0:T(8,128)(2,1)} %get-tuple-element.25) | copy-start | bytes 786436
